TPU v7x, 32 devices: a whole 2x2x4 slice. The times are simulated.
32 devices in a mesh: seq: 8 (over z, y), head: 4 (over x, core).
Axes of the slice: x: 2, y: 2, z: 4, core: 2. Of those that a mesh axis runs over, the one named last changes fastest.
Arguments:
- hidden_in: bfloat16 [2, 16384, 768], P(None, 'seq'), may hold values from -6 to 6
- output_cotangent: bfloat16 [2, 16384, 768], P(None, 'seq', 'head'), may hold values from -6 to 6
- input_norm_scale_gain: float32 [768], replicated, may hold values from 0.5 to 1.5
- z_proj: bfloat16 [768, 1536], P(None, 'head'), may hold values from -0.21875 to 0.21875
- x_proj: bfloat16 [768, 1536], P(None, 'head'), may hold values from -0.21875 to 0.21875
- bc_proj: bfloat16 [768, 256], replicated, may hold values from -0.21875 to 0.21875
- dt_proj: bfloat16 [768, 24], P(None, 'head'), may hold values from -0.21875 to 0.21875
- conv_x_weight: float32 [1536, 4], P('head'), may hold values from -3 to 3
- conv_x_bias: float32 [1536], P('head'), may hold values from -1.2 to 1.2
- conv_bc_weight: float32 [256, 4], replicated, may hold values from -3 to 3
- conv_bc_bias: float32 [256], replicated, may hold values from -1.2 to 1.2
- dt_bias: float32 [24], P('head'), may hold values from -2 to 0.5
- a_log: float32 [24], P('head')
- d_skip: float32 [24], P('head'), may hold values from 0.5 to 1.5
- out_norm_gain: float32 [1536], P('head'), may hold values from 0.5 to 1.5
- out_proj: bfloat16 [1536, 768], P('head'), may hold values from -0.15625 to 0.15625
- doc_starts: int32 [2, 84], replicated, may hold values from 0 to 16384, as said below
Outputs:
- layer_out: bfloat16 [2, 16384, 768], P(None, 'seq', 'head')
- input_grad: bfloat16 [2, 16384, 768], P(None, 'seq', 'head')
- grad_in_norm_gain: float32 [768], P('head')
- grad_z_proj: float32 [768, 1536], P(None, 'head')
- grad_x_proj: float32 [768, 1536], P(None, 'head')
- grad_bc_proj: float32 [768, 256], replicated
- grad_dt_proj: float32 [768, 24], P(None, 'head')
- grad_conv_x_weight: float32 [1536, 4], P('head')
- grad_conv_x_bias: float32 [1536], P('head')
- grad_conv_bc_weight: float32 [256, 4], replicated
- grad_conv_bc_bias: float32 [256], replicated
- grad_dt_bias: float32 [24], P('head')
- grad_a_log: float32 [24], P('head')
- grad_d_skip: float32 [24], P('head')
- grad_out_norm_gain: float32 [1536], P('head')
- grad_out_proj: float32 [1536, 768], P('head')
Inputs may be any that keep to these rules, and one draw needn't show every extreme that they name: doc_starts[b] holds the first positions of sequence b's documents in rising order, beginning with 0; every slot after the last document holds 16384.
All inputs are finite; a program needn't handle non-finite values.
Results may differ from a plain program's by a relative error of at most 0.0075.
The roundings to bfloat16 on the way count: a program that leaves them out, or rounds other values in their place, can miss the bound.
Values may be sent and summed in bfloat16 or wider, within the bound.
A program may use at most 256 MiB of HBM per device.

v0:
```python
import functools

import jax
import jax.numpy as jnp
import numpy as np
from jax import lax
from jax.experimental import pallas as pl
from jax.experimental.pallas import tpu as pltpu
from jax.sharding import PartitionSpec as P

GROUP = 256
HALF = 128
LANES = 128
HEAD_DIM = 64
EPS = 1e-05
LOG2E = 1.4426950408889634
f32 = jnp.float32
bf16 = jnp.bfloat16
HIGHEST = lax.Precision.HIGHEST
ROWS = 32
MESH = pl.DeviceIdType.MESH


def dot(a, b, ca=1, cb=0, precision=None):
    return lax.dot_general(
        a, b, (((ca,), (cb,)), ((), ())), precision=precision, preferred_element_type=f32
    )


def split2(x):
    hi = x.astype(bf16)
    return hi, (x - hi.astype(f32)).astype(bf16)


def pack(x):
    hi = x.astype(bf16).astype(f32)
    rest = x - hi
    mid = rest.astype(bf16).astype(f32)
    return (hi + pltpu.roll(mid, 32, 1) + pltpu.roll(rest - mid, 64, 1)).astype(bf16)


def unpack(x):
    x = x.astype(f32)
    return lanes_below(x + pltpu.roll(x, LANES - 32, 1) + pltpu.roll(x, LANES - 64, 1), 12)


def expand(x, ex):
    return dot(pack(x), ex)


def lanes_below(x, count):
    return jnp.where(lax.broadcasted_iota(jnp.int32, x.shape, 1) < count, x, 0.0)


def sigmoid(x):
    return 1.0 / (1.0 + jnp.exp(-x))


def softplus(x):
    return jnp.maximum(x, 0.0) + jnp.log1p(jnp.exp(-jnp.abs(x)))


def fold8(x):
    total = x[0:8]
    for r in range(8, x.shape[0], 8):
        total = total + x[r : r + 8]
    return total


def expansion(width):
    heads = width // HEAD_DIM
    ex = np.zeros((LANES, width), np.float32)
    for part in range(3):
        for h in range(heads):
            ex[32 * part + h, h * HEAD_DIM : (h + 1) * HEAD_DIM] = 1.0
    red = np.zeros((width, LANES), np.float32)
    for h in range(heads):
        red[h * HEAD_DIM : (h + 1) * HEAD_DIM, h] = 1.0
    return jnp.asarray(ex, bf16), jnp.asarray(red, bf16)


def run(kernel, grid, ins, outs, scratch=(), flops=0, moved=0, prefetch=(), collective=None):
    def spec(shape, block, imap):
        if block is pl.ANY:
            return pl.BlockSpec(memory_space=pl.ANY)
        if block is None:
            rank = len(shape)
            return pl.BlockSpec(shape, lambda *_: (0,) * rank)
        return pl.BlockSpec(block, imap)

    extra = {} if collective is None else {"collective_id": collective, "has_side_effects": True}
    return pl.pallas_call(
        kernel,
        grid_spec=pltpu.PrefetchScalarGridSpec(
            num_scalar_prefetch=len(prefetch),
            grid=grid,
            in_specs=[spec(a.shape, b, m) for a, b, m in ins],
            out_specs=[spec(s, b, m) for s, _, b, m in outs],
            scratch_shapes=list(scratch),
        ),
        out_shape=[jax.ShapeDtypeStruct(s, d) for s, d, _, _ in outs],
        compiler_params=pltpu.CompilerParams(vmem_limit_bytes=56 << 20, **extra),
        cost_estimate=pl.CostEstimate(flops=flops, bytes_accessed=moved, transcendentals=0),
    )(*prefetch, *[a for a, _, _ in ins])


def conv_rows(ext, age, taps, bias, r, cols):
    acc = jnp.broadcast_to(bias[:, cols], (ROWS, LANES))
    for k in range(4):
        back = 3 - k
        term = ext[8 + r - back : 8 + r - back + ROWS, cols] * taps[k : k + 1, cols]
        if back:
            term = jnp.where(age >= back, term, 0.0)
        acc = acc + term
    return acc


def rms(x, gain):
    x = x.astype(f32)
    r = lax.rsqrt(jnp.sum(x * x, axis=1, keepdims=True) / x.shape[1] + EPS)
    return (x * r * gain).astype(bf16)


def spread_ages(starts, first, rows):
    token = first + lax.broadcasted_iota(jnp.int32, (rows, starts.shape[1]), 0)
    begun = jnp.where(starts <= token, starts, 0).astype(f32)
    begun = jnp.max(begun, axis=1, keepdims=True).astype(jnp.int32)
    place = first + lax.broadcasted_iota(jnp.int32, (rows, LANES), 0)
    return place - begun


def front_step(
    with_maps, i, normed, before, wa, wb, sa, sb, age, tril, ex, maps_in,
    ci, co, val, pre, cum, lin, kb, ck, tot, kout, par, dtp, maps_out,
    ext, running, kept, omx, ohi, olo, dts, ext_bc,
):
    width = val.shape[1]
    part = width // 2
    heads = part // HEAD_DIM
    if with_maps:
        ci_bc, bc, taps_bc, bias_bc = maps_in
        bias_bc = bias_bc[0:1]
        co_bc, bmat, cmat = maps_out
    else:
        (bmat,) = maps_in

    @pl.when(i == 0)
    def _():
        running[...] = jnp.zeros_like(running)
        kept[...] = jnp.ones_like(kept)
        for w, at in ((wa, 0), (wb, part)):
            ext[0:8, at : at + part] = dot(before[...], w[...]).astype(bf16).astype(f32)[8:16]
        if with_maps:
            ext_bc[0:8] = dot(before[...], bc[...]).astype(bf16).astype(f32)[8:16]
        par[...] = jnp.zeros_like(par)
        for s, at in ((sa, 0), (sb, part)):
            par[0:6, at : at + part] = s[0:6, :part]
        rows_a, rows_b = (jnp.broadcast_to(s[6:7, 0:LANES], (8, LANES)) for s in (sa, sb))

        def lanes(k):
            a = lanes_below(pltpu.roll(rows_a, (LANES - k * heads) % LANES, 1), heads)
            b = lanes_below(pltpu.roll(rows_b, (LANES - k * heads) % LANES, 1), heads)
            return a + pltpu.roll(b, heads, 1)

        par[7:8, LANES : 2 * LANES] = lanes(0)[0:1]
        par[7:8, 0:LANES] = -jnp.exp(lanes(1)[0:1])
        par[6:7] = expand(lanes(2), ex[...])[0:1]
        dts[...] = jnp.zeros_like(dts)
        dts[0:heads] = sa[8 : 8 + heads]
        dts[heads : 2 * heads] = sb[8 : 8 + heads]
        dtp[...] = dts[...].astype(bf16)

    @pl.when(i > 0)
    def _():
        ext[0:8] = ext[GROUP : GROUP + 8]
        if with_maps:
            ext_bc[0:8] = ext_bc[GROUP : GROUP + 8]

    taps, bias = par, par[4:5]
    rate, dtb = par[7:8, 0:LANES], par[7:8, LANES : 2 * LANES]
    for w, at in ((wa, 0), (wb, part)):
        low = dot(normed[...], w[...]).astype(bf16)
        ci[:, at : at + part] = low
        ext[8 : 8 + GROUP, at : at + part] = low.astype(f32)
    raw = dot(normed[...], dtp[...], 1, 1) + dtb
    pre[...] = raw
    delta = softplus(raw)
    c = dot(tril[...], delta * rate, precision=HIGHEST)
    cum[...] = c
    end = c[GROUP - 1 : GROUP]
    age_end = age[GROUP - 1 : GROUP]
    left = GROUP - 1 - lax.broadcasted_iota(jnp.int32, c.shape, 0)
    omega = jnp.where(left <= age_end, jnp.exp(end - c), 0.0) * delta
    omx[...] = expand(lanes_below(omega, 2 * heads), ex[...])
    keep = jnp.where(age_end >= GROUP, jnp.exp(end), 0.0)
    keep = lanes_below(jnp.broadcast_to(keep, (8, LANES)), 2 * heads)
    keepx = expand(keep, ex[...])
    if with_maps:
        ext_bc[8 : 8 + GROUP] = ci_bc[...].astype(f32)
        for r in range(0, GROUP, ROWS):
            a = age[r : r + ROWS]
            for j, out in enumerate((bmat, cmat)):
                cols = slice(j * LANES, (j + 1) * LANES)
                v = conv_rows(ext_bc, a, taps_bc, bias_bc, r, cols)
                co_bc[r : r + ROWS, cols] = v
                out[r : r + ROWS] = (v * sigmoid(v)).astype(bf16)
    for r in range(0, GROUP, ROWS):
        a = age[r : r + ROWS]
        rows = slice(r, r + ROWS)
        for j in range(width // LANES):
            cols = slice(j * LANES, (j + 1) * LANES)
            v = conv_rows(ext, a, taps, bias, r, cols)
            co[rows, cols] = v
            act = (v * sigmoid(v)).astype(bf16)
            val[rows, cols] = act
            ohi[rows, cols], olo[rows, cols] = split2(omx[rows, cols] * act.astype(f32))
    own = dot(bmat[...], ohi[...], 0, 0) + dot(bmat[...], olo[...], 0, 0)
    lin[0] = running[...]
    kb[0] = expand(lanes_below(kept[...], 2 * heads), ex[...])
    ck[0] = keepx
    running[...] = keepx[0:1] * running[...] + own
    kept[...] = keep * kept[...]
    tot[...] = running[...]
    kout[...] = kept[...]


def head_peers():
    head = lax.axis_index("head")
    near = head + 1 - 2 * lax.rem(head, 2)
    return [head, near, lax.rem(head + 2, 4), lax.rem(near + 2, 4)]


def meet(heads, n, extra=0):
    me = lax.axis_index("seq")
    barrier = pltpu.get_barrier_semaphore()
    for head in heads:
        pl.semaphore_signal(barrier, inc=1, device_id={"head": head}, device_id_type=MESH)
    for d in range(1, n):
        pl.semaphore_signal(barrier, inc=1, device_id={"seq": lax.rem(me + d, n)}, device_id_type=MESH)
    pl.semaphore_wait(barrier, n - 1 + len(heads))


def send(src, dst, sems, k, device):
    return pltpu.make_async_remote_copy(
        src_ref=src, dst_ref=dst, send_sem=sems.at[0, k], recv_sem=sems.at[1, k],
        device_id=device, device_id_type=MESH,
    )


class Weights:
    def __init__(self, n, own, outs, scratch):
        self.own, self.outs = own, outs
        self.near, self.far, self.far_near, self.sems = scratch
        me = lax.axis_index("seq")
        odd = lax.rem(me, 2)
        heads = head_peers()
        half = own.shape[0] // 2
        rows = pl.ds(pl.multiple_of(odd * half, half), half)
        near, mate = {"head": heads[1]}, {"seq": me + 1 - 2 * odd}
        self.copies = [
            send(own, self.near, self.sems, 0, near),
            send(own.at[rows], self.far.at[rows], self.sems, 1, {"head": heads[2]}),
            send(self.far.at[rows], self.far.at[rows], self.sems, 2, mate),
            send(self.far, self.far_near, self.sems, 3, near),
        ]

    @staticmethod
    def scratch(rows, cols):
        return [pltpu.VMEM((rows, cols), bf16)] * 3 + [pltpu.SemaphoreType.DMA((2, 4))]

    def begin(self):
        self.copies[1].start()
        self.copies[0].start()

    def share(self):
        self.copies[1].wait()
        self.copies[2].start()

    def back(self):
        self.copies[2].wait()
        self.copies[3].start()

    def finish(self):
        self.copies[0].wait()
        self.copies[3].wait()
        for to, x in zip(self.outs, (self.near, self.far, self.far_near)):
            to[...] = x[...]


def cot_copies(cotangent, outs, which, parts, sems):
    heads = head_peers()
    copies = []
    for k, out in zip(which, outs):
        chunk = out.shape[1]
        cols = pl.ds(pl.multiple_of(lax.rem(heads[k], parts) * chunk, chunk), chunk)
        copies.append(send(cotangent.at[heads[k] // parts, :, cols], out, sems, k, {"head": heads[k]}))
    return copies


class Exchange:
    def __init__(self, reverse, n, parts, tots, kouts, ex, own, other, scratch):
        self.reverse, self.n, self.tots, self.kouts, self.ex = reverse, n, tots, kouts, ex
        self.own, self.other = own, other
        (
            self.out, self.got, self.payload, self.spread, self.scanned, self.home, self.lead, self.lead_k, self.arr,
            self.theirs, self.last, self.swap_sems, self.to_sems, self.from_sems, self.back_to, self.back_from,
        ) = scratch
        self.me = lax.axis_index("seq")
        head = lax.axis_index("head")
        self.partner = head + 1 - 2 * lax.rem(head, 2)
        half = lax.rem(head, parts)
        self.leads = (half if reverse else 1 - half).astype(f32)
        self.per = LANES // n

    @staticmethod
    def scratch(n, width):
        rows = max(LANES // n, 8)
        return [
            pltpu.VMEM((LANES + 8, width), f32),
            pltpu.VMEM((LANES + 8, width), f32),
            pltpu.VMEM((n, rows, width + LANES), f32),
            pltpu.VMEM((n, rows, width + LANES), f32),
            pltpu.VMEM((n, rows, width), f32),
            pltpu.VMEM((n, rows, width), f32),
            pltpu.VMEM((LANES, width), f32),
            pltpu.VMEM((8, LANES), f32),
            pltpu.VMEM((LANES, width), f32),
            pltpu.VMEM((LANES, width), f32),
            pltpu.VMEM((LANES, width), f32),
            pltpu.SemaphoreType.DMA((4,)),
            pltpu.SemaphoreType.DMA((n,)),
            pltpu.SemaphoreType.DMA((n,)),
            pltpu.SemaphoreType.DMA((n,)),
            pltpu.SemaphoreType.DMA((n,)),
        ]

    def peers(self):
        for d in range(1, self.n):
            yield d, lax.rem(self.me + d, self.n), lax.rem(self.me + self.n - d, self.n)

    def swap(self, src, dst, sem):
        return pltpu.make_async_remote_copy(
            src_ref=src,
            dst_ref=dst,
            send_sem=self.swap_sems.at[sem],
            recv_sem=self.swap_sems.at[sem + 1],
            device_id={"head": self.partner},
            device_id_type=MESH,
        )

    def move(self, src, dst, d, to, send_sems, recv_sems):
        return pltpu.make_async_remote_copy(
            src_ref=src.at[to],
            dst_ref=dst.at[self.me],
            send_sem=send_sems.at[d],
            recv_sem=recv_sems.at[d],
            device_id={"seq": to},
            device_id_type=MESH,
        )

    def begin(self):
        part = self.tots[0].shape[1] // 2
        heads = part // HEAD_DIM
        for k in range(len(self.tots)):
            self.out[0:LANES, k * part : (k + 1) * part] = self.tots[k][:, part:]
            rolled = pltpu.roll(self.kouts[k][...], LANES - heads, 1)
            self.out[LANES : LANES + 8, k * LANES : (k + 1) * LANES] = lanes_below(rolled, heads)
        used = len(self.tots) * LANES
        self.out[LANES : LANES + 8, used:] = jnp.zeros((8, self.out.shape[1] - used), f32)
        self.swap(self.out, self.got, 0).start()

    def combine(self):
        self.swap(self.out, self.got, 0).wait()
        part = self.tots[0].shape[1] // 2
        heads = part // HEAD_DIM
        width = len(self.tots) * part
        leads, follows = self.leads, 1.0 - self.leads
        mine_k, got_k = jnp.zeros((8, LANES), f32), jnp.zeros((8, LANES), f32)
        for k, kout in enumerate(self.kouts):
            both = (lanes_below(kout[...], heads), self.got[LANES : LANES + 8, k * LANES : (k + 1) * LANES])
            both = [pltpu.roll(x, k * heads, 1) if k else x for x in both]
            mine_k, got_k = mine_k + both[0], got_k + both[1]
        lk = leads * mine_k + follows * got_k
        fk = leads * got_k + follows * mine_k
        fkx = expand(fk, self.ex[:, :width])[0:1]
        self.lead_k[...] = lk
        for k in range(len(self.tots)):
            cols = slice(k * part, (k + 1) * part)
            mine, got = self.tots[k][:, :part], self.got[0:LANES, cols]
            ls = leads * mine + follows * got
            self.lead[:, cols] = ls
            self.arr[:, cols] = fkx[:, cols] * ls + (leads * got + follows * mine)
        keep = (lk * fk)[0:1]
        rows = self.payload.shape[1]
        for s in range(self.n):
            self.payload[s, 0 : self.per, 0:width] = self.arr[s * self.per : (s + 1) * self.per]
            self.payload[s, :, width:] = jnp.broadcast_to(keep, (rows, LANES))
        for d, to, _ in self.peers():
            self.move(self.payload, self.spread, d, to, self.to_sems, self.from_sems).start()
        self.spread[self.me] = self.payload[self.me]

    def scan(self):
        for d, to, _ in self.peers():
            self.move(self.payload, self.spread, d, to, self.to_sems, self.from_sems).wait()
        width = self.scanned.shape[2]
        rows = self.scanned.shape[1]
        state = jnp.zeros((rows, width), f32)
        for step in range(self.n):
            at = self.n - 1 - step if self.reverse else step
            self.scanned[at] = state
            if step < self.n - 1:
                keep = expand(self.spread[at, :, width:], self.ex[:, :width])
                state = keep * state + self.spread[at, :, 0:width]
        for d, to, _ in self.peers():
            self.move(self.scanned, self.home, d, to, self.back_to, self.back_from).start()
        self.home[self.me] = self.scanned[self.me]

    def settle(self):
        for d, to, _ in self.peers():
            self.move(self.scanned, self.home, d, to, self.back_to, self.back_from).wait()
        for s in range(self.n):
            self.arr[s * self.per : (s + 1) * self.per] = self.home[s, 0 : self.per]
        leads, follows = self.leads, 1.0 - self.leads
        first = self.arr[...]
        second = expand(self.lead_k[...], self.ex[:, : first.shape[1]])[0:1] * first + self.lead[...]
        self.theirs[...] = leads * second + follows * first
        self.swap(self.theirs, self.last, 2).start()
        self.own[...] = leads * first + follows * second

    def close(self):
        self.swap(self.theirs, self.last, 2).wait()
        self.other[...] = self.last[...]


def pair_masks(x, lane_axis_shape):
    lane = lax.broadcasted_iota(jnp.int32, lane_axis_shape, 1)
    zero = jnp.zeros_like(x)
    return jnp.where(lane < HEAD_DIM, x, zero), jnp.where(lane >= HEAD_DIM, x, zero)


def intra_unit(val, bmat, cmat, age, pre, cum, dskip, part):
    t = lax.broadcasted_iota(jnp.int32, (HALF, HALF), 0)
    s = lax.broadcasted_iota(jnp.int32, (HALF, HALF), 1)
    scores = dot(cmat[...], bmat[...], 1, 1)
    a0, a1 = age[0:HALF], age[HALF:]
    gap = t - s
    s00 = jnp.where((gap >= 0) & (gap <= a0), scores[:HALF, :HALF], 0.0)
    s11 = jnp.where((gap >= 0) & (gap <= a1), scores[HALF:, HALF:], 0.0)
    s10 = jnp.where(gap + HALF <= a1, scores[HALF:, :HALF], 0.0)
    c2 = cum[...] * LOG2E
    rows = (c2 - jnp.log2(softplus(pre[...]))).T
    for j in range(val.shape[1] // LANES):
        cols = slice(j * LANES, (j + 1) * LANES)
        v = val[:, cols]
        vm = pair_masks(v, v.shape)
        tops, bottoms = [], []
        for which in range(2):
            h = 2 * j + which
            col0 = jnp.broadcast_to(c2[:HALF, h : h + 1], (HALF, HALF))
            col1 = jnp.broadcast_to(c2[HALF:, h : h + 1], (HALF, HALF))
            r0 = rows[h : h + 1, :HALF]
            r1 = rows[h : h + 1, HALF:]
            tops.append((s00 * jnp.exp2(jnp.minimum(col0 - r0, 60.0))).astype(bf16))
            bottoms.append((s10 * jnp.exp2(col1 - r0)).astype(bf16))
            bottoms.append((s11 * jnp.exp2(jnp.minimum(col1 - r1, 60.0))).astype(bf16))
        top = dot(jnp.concatenate(tops, axis=1), jnp.concatenate([vm[0][:HALF], vm[1][:HALF]], axis=0))
        bottom = dot(jnp.concatenate(bottoms, axis=1), jnp.concatenate([vm[0], vm[1]], axis=0))
        skip = dskip[6:7, cols]
        part[:HALF, cols] = top + skip * v[:HALF].astype(f32)
        part[HALF:, cols] = bottom + skip * v[HALF:].astype(f32)


def forward_kernel(
    n, parts, count, hid, tail_rows, edge_near, starts, vecs, taps_x, dt_own, x_own, z_own, o_own, bc, taps_bc,
    tril, ex, cotangent,
    normed, ci_bc, age, ager, next_age, gain_out, x_near, x_far, x_far_near, z_near, z_far, z_far_near,
    o_near, o_far, o_far_near, cot_near, cot_across, cot_corner, co_bc, bmat, cmat, *refs,
):
    (ci_a, co_a, val_a, pre_a, cum_a, lin_a, kb_a, ck_a, par_a, dtp_a, own_a, other_a, part_a), refs = refs[:13], refs[13:]
    (ci_b, co_b, val_b, pre_b, cum_b, lin_b, kb_b, ck_b, par_b, dtp_b, own_b, other_b, part_b), refs = refs[:13], refs[13:]
    (
        gain, bias_bc, before, edge_far, small_s, small_n, small_f, small_fn, xn, xf, xfn,
        tot_a, tot_b, kout_a, kout_b, sems, cot_sems,
    ), refs = refs[:17], refs[17:]
    front, refs = refs[:8], refs[8:]
    z_weights = Weights(n, z_own, (z_near, z_far, z_far_near), refs[:4])
    o_weights = Weights(n, o_own, (o_near, o_far, o_far_near), refs[4:8])
    refs = refs[8:]
    size = len(refs) // 2
    states_a = Exchange(False, n, parts, (tot_a,), (kout_a,), ex, own_a, other_a, refs[:size])
    states_b = Exchange(False, n, parts, (tot_b,), (kout_b,), ex, own_b, other_b, refs[size:])
    cots = cot_copies(cotangent, (cot_near, cot_across, cot_corner), (1, 2, 3), parts, cot_sems)
    u = pl.program_id(0)
    s_me = lax.axis_index("seq")
    heads = head_peers()
    near, across = {"head": heads[1]}, {"head": heads[2]}
    half = lax.rem(heads[0], parts)
    batch = heads[0] // parts
    chunk = count * GROUP
    features = bc.shape[0]
    part = x_own.shape[1]
    nh = dt_own.shape[0]
    first = (s_me * parts + half) * chunk
    row = starts[0:1]
    for b in range(1, starts.shape[0]):
        row = jnp.where(batch == b, starts[b : b + 1], row)

    swap_x = send(x_own, xn, sems, 0, near)
    swap_small = send(small_s, small_n, sems, 1, near)
    cross_x = send(x_own, xf, sems, 2, across)
    cross_small = send(small_s, small_f, sems, 3, across)
    swap_far = send(xf, xfn, sems, 4, near)
    swap_small_far = send(small_f, small_fn, sems, 5, near)
    edge = send(tail_rows.at[0], edge_far, sems, 6, {"seq": lax.min(s_me + 1, n - 1)})

    @pl.when(u == 0)
    def _():
        small_s[...] = jnp.zeros_like(small_s)
        small_s[0:4, 0:part] = taps_x[...]
        tiles = part // LANES
        for k in range(tiles):
            cols = slice(k * LANES, (k + 1) * LANES)
            small_s[4:5, cols] = vecs[k : k + 1]
            small_s[5:6, cols] = vecs[tiles + k : tiles + k + 1]
        small_s[6:7, 0:LANES] = vecs[2 * tiles : 2 * tiles + 1]
        small_s[8 : 8 + nh] = dt_own[...].astype(f32)
        at = 2 * tiles + 2
        for k in range(features // LANES):
            gain[0:1, k * LANES : (k + 1) * LANES] = vecs[at + k : at + k + 1]
        at = at + features // LANES
        for k in range(2):
            bias_bc[0:1, k * LANES : (k + 1) * LANES] = vecs[at + k : at + k + 1]
        gain_out[...] = jnp.broadcast_to(gain[0:1], gain_out.shape)
        edge_far[...] = jnp.zeros_like(edge_far)
        meet(heads[1:], n)
        swap_small.start()
        swap_x.start()
        pl.when(s_me < n - 1)(edge.start)
        cross_small.start()
        cross_x.start()
        next_age[...] = spread_ages(row, first + chunk, 8)

    rows = pl.ds(pl.multiple_of(lax.rem(u, count) * GROUP, GROUP), GROUP)

    @pl.when(u < count)
    def _():
        for r in range(0, GROUP, ROWS):
            at = pl.ds(pl.multiple_of(u * GROUP + r, ROWS), ROWS)
            normed[at] = rms(hid[0, r : r + ROWS], gain[0:1])
        ci_bc[rows] = dot(normed[rows], bc[...]).astype(bf16)
        a = spread_ages(row, first + u * GROUP, GROUP)
        age[rows] = a
        ager[...] = a.astype(f32).T[0:8].astype(jnp.int32)

    @pl.when(u == count)
    def _():
        swap_small.wait()
        swap_x.wait()
        pl.when(s_me < n - 1)(edge.wait_send)
        pl.when(s_me > 0)(edge.wait_recv)
        local = half.astype(f32)
        near_rows = local * edge_near[0].astype(f32) + (1.0 - local) * edge_far[...].astype(f32)
        before[...] = rms(near_rows, gain[0:1])

    @pl.when(u == 2 * count - 1)
    def _():
        cross_small.wait()
        swap_small_far.start()
        cross_x.wait()
        swap_far.start()
        z_weights.begin()

    @pl.when(u == 2 * count)
    def _():
        states_a.begin()
        swap_small_far.wait()
        swap_far.wait()
        x_near[...] = xn[...]
        x_far[...] = xf[...]
        x_far_near[...] = xfn[...]

    pl.when(u == 2 * count + 1)(states_a.combine)

    @pl.when(u == 2 * count + 2)
    def _():
        z_weights.share()
        o_weights.begin()

    pl.when(u == 2 * count + 3)(states_a.scan)

    @pl.when(u == 3 * count)
    def _():
        states_b.begin()
        z_weights.back()
        for copy in cots:
            copy.start()

    @pl.when(u == 3 * count + 1)
    def _():
        states_b.combine()
        o_weights.share()

    pl.when(u == 3 * count + 2)(states_a.settle)
    pl.when(u == 3 * count + 4)(states_a.close)

    @pl.when(u == 5 * count - 3)
    def _():
        states_b.scan()
        o_weights.back()

    for which in range(2):
        lo = (which + 1) * count
        outs = (ci_a, co_a, val_a, pre_a, cum_a, lin_a, kb_a, ck_a, tot_a, kout_a, par_a, dtp_a)
        weights = (x_own, xn, small_s, small_n)
        maps_in, maps_out = (ci_bc.at[rows], bc, taps_bc, bias_bc), (co_bc, bmat.at[rows], cmat.at[rows])
        if which:
            outs = (ci_b, co_b, val_b, pre_b, cum_b, lin_b, kb_b, ck_b, tot_b, kout_b, par_b, dtp_b)
            weights = (xf, xfn, small_f, small_fn)
            maps_in, maps_out = (bmat.at[rows],), ()
        outs = outs[:2] + tuple(x.at[rows] for x in outs[2:5]) + outs[5:]

        @pl.when((u >= lo) & (u < lo + count))
        def _():
            front_step(
                which == 0, u - lo, normed.at[rows], before, *weights, age.at[rows], tril, ex,
                maps_in, *outs, maps_out, *front,
            )

    for which in range(2):
        lo = (which + 3) * count
        val, pre, cum, par, to = ((val_a, pre_a, cum_a, par_a, part_a), (val_b, pre_b, cum_b, par_b, part_b))[which]

        @pl.when((u >= lo) & (u < lo + count))
        def _():
            intra_unit(
                val.at[rows], bmat.at[rows], cmat.at[rows], age.at[rows], pre.at[rows], cum.at[rows], par, to
            )

    @pl.when(u == 5 * count - 1)
    def _():
        z_weights.finish()
        o_weights.finish()
        states_b.settle()
        for copy in cots:
            copy.wait()
        states_b.close()


def arriving_half(own, other, half=None):
    if half is None:
        return jnp.concatenate([own[...], other[...]], axis=1)
    part = own.shape[1] // 2
    cols = slice(half * part, (half + 1) * part)
    return jnp.concatenate([own[:, cols].astype(f32), other[:, cols].astype(f32)], axis=1)


def mid_kernel(
    meta, hid, normed, z0, z1, z2, z3, o0, o1, o2, o3, cot0, cot1, cot2, cot3, cmat, age, ex, red, par_a, par_b,
    part_a, part_b, val_a, val_b, cum_a, cum_b, lin_a, lin_b, kb_a, kb_b, ck_a, ck_b, arr_a, arr_other_a, arr_b, arr_other_b,
    pieces, hidc, nout, cotx, dssd, dgate, dcin, dkk_a, dkk_b,
    lout_a, lout_b, ka_a, ka_b, tot_a, tot_b, kout_a, kout_b, ggain, gskip,
    gate, dno, read, kx, ssd_s, sig_s, khi, klo, rhi, rlo, run_a, run_b, kept_a, kept_b, shuffle,
):
    i = pl.program_id(0)
    inner = nout.shape[1]
    width = inner // 2
    tiles = inner // LANES
    heads = width // HEAD_DIM
    quarter = inner // 4

    @pl.when(i == 0)
    def _():
        for ref in (run_a, run_b, ggain, gskip):
            ref[...] = jnp.zeros_like(ref)
        for ref in (kept_a, kept_b):
            ref[...] = jnp.ones_like(ref)

    me = meta[0]
    hidc[...] = hid[0]
    for k, cot in enumerate((cot0.at[0], cot1, cot2, cot3)):
        shuffle[me ^ k] = cot[...]
    cotan = jnp.concatenate([shuffle[0], shuffle[1], shuffle[2], shuffle[3]], axis=0).T
    cotx[...] = cotan
    states = []
    for half, (lin, kb, cum, arr, arr_other) in enumerate(
        ((lin_a, kb_a, cum_a, arr_a, arr_other_a), (lin_b, kb_b, cum_b, arr_b, arr_other_b))
    ):
        cols = slice(half * width, (half + 1) * width)
        hi, lo = split2(lin[0] + kb[0, 0:1] * arriving_half(arr, arr_other))
        states.append((hi, lo))
        read[:, cols] = dot(cmat[...], hi) + dot(cmat[...], lo)
        since = lax.broadcasted_iota(jnp.int32, age.shape, 0)
        kappa = jnp.where(age[...] > since, jnp.exp(cum[...]), 0.0)
        kx[:, cols] = expand(lanes_below(kappa, heads), ex[...])
    for k, (z, o) in enumerate(((z0, o0), (z1, o1), (z2, o2), (z3, o3))):
        cols = slice(k * quarter, (k + 1) * quarter)
        gate[:, cols] = dot(normed[...], z[...])
        dno[:, cols] = dot(cotan, o[...], 1, 1)

    gains = [
        (par_a if j < tiles // 2 else par_b)[5:6, (j * LANES) % width : (j * LANES) % width + LANES]
        for j in range(tiles)
    ]

    def rows_body(step, _):
        rows = pl.ds(pl.multiple_of(step * ROWS, ROWS), ROWS)
        squares = jnp.zeros((ROWS, LANES), f32)
        inners = jnp.zeros((ROWS, LANES), f32)
        for j in range(tiles):
            cols = slice(j * LANES, (j + 1) * LANES)
            part = part_a if j < tiles // 2 else part_b
            pcols = slice(cols.start % width, cols.start % width + LANES)
            ssd = part[rows, pcols] + kx[rows, cols] * read[rows, cols]
            g = gate[rows, cols]
            sig = sigmoid(g)
            gated = ssd * (g * sig)
            squares += gated * gated
            inners += gated * (dno[rows, cols] * gains[j])
            ssd_s[rows, cols] = ssd
            sig_s[rows, cols] = sig
        rg = lax.rsqrt(jnp.sum(squares, axis=1, keepdims=True) / inner + EPS)
        stat = rg * rg * (jnp.sum(inners, axis=1, keepdims=True) / inner)
        rg = jnp.broadcast_to(rg, (ROWS, LANES))
        stat = jnp.broadcast_to(stat, (ROWS, LANES))
        for j in range(tiles):
            cols = slice(j * LANES, (j + 1) * LANES)
            val = val_a if j < tiles // 2 else val_b
            pcols = slice(cols.start % width, cols.start % width + LANES)
            ssd, sig, g, d = ssd_s[rows, cols], sig_s[rows, cols], gate[rows, cols], dno[rows, cols]
            act = g * sig
            gated = ssd * act
            yhat = gated * rg
            nout[rows, cols] = (yhat * gains[j]).astype(bf16)
            ggain[:, cols] += fold8(d * yhat)
            dgated = rg * (d * gains[j] - gated * stat)
            low = (dgated * act).astype(bf16)
            dssd[rows, cols] = low
            dgate[rows, cols] = (dgated * ssd * (sig * (1.0 + g * (1.0 - sig)))).astype(bf16)
            dy = low.astype(f32)
            gskip[:, cols] += fold8(dy * val[rows, pcols].astype(f32))
            kd = kx[rows, cols] * dy
            khi[rows, cols], klo[rows, cols] = split2(kd)
            rhi[rows, cols], rlo[rows, cols] = split2(kd * read[rows, cols])
        return 0

    lax.fori_loop(0, GROUP // ROWS, rows_body, 0)
    out = hid[0].astype(f32)
    for k, o in enumerate((o0, o1, o2, o3)):
        out = out + dot(nout[:, k * quarter : (k + 1) * quarter], o[...])
    out = out.astype(bf16).T
    piece = out.shape[0] // 4
    for k in range(4):
        pieces[k] = out[k * piece : (k + 1) * piece]
    dc = None
    age_end = age[GROUP - 1 : GROUP]
    for half, (dkk, ck, cum, lout, ka, tot, kout, running, kept) in enumerate(
        (
            (dkk_a, ck_a, cum_a, lout_a, ka_a, tot_a, kout_a, run_a, kept_a),
            (dkk_b, ck_b, cum_b, lout_b, ka_b, tot_b, kout_b, run_b, kept_b),
        )
    ):
        cols = slice(half * width, (half + 1) * width)
        hi, lo = states[half]
        dkk[...] = dot(rhi[:, cols], red[...]) + dot(rlo[:, cols], red[...])
        term = dot(khi[:, cols], hi, 1, 1) + dot(khi[:, cols], lo, 1, 1) + dot(klo[:, cols], hi, 1, 1)
        dc = term if dc is None else dc + term
        own = dot(cmat[...], khi[:, cols], 0, 0) + dot(cmat[...], klo[:, cols], 0, 0)
        lout[0] = running[...]
        ka[0] = expand(lanes_below(kept[...], heads), ex[...])
        running[...] = ck[0, 0:1] * running[...] + own
        keep = jnp.where(age_end >= GROUP, jnp.exp(cum[GROUP - 1 : GROUP]), 0.0)
        kept[...] = lanes_below(jnp.broadcast_to(keep, (8, LANES)), heads) * kept[...]
        tot[...] = running[...]
        kout[...] = kept[...]
    dcin[...] = dc


def pairs_unit(val, dssd, bmat, cmat, ager, pre, cum, dvi, dbi, dci, rflow, cflow, rft):
    s = lax.broadcasted_iota(jnp.int32, (HALF, HALF), 0)
    t = lax.broadcasted_iota(jnp.int32, (HALF, HALF), 1)
    scores = dot(bmat[...], cmat[...], 1, 1)
    a0, a1 = ager[0:1, :HALF], ager[0:1, HALF:]
    gap = t - s
    m00 = (gap >= 0) & (gap <= a0)
    m11 = (gap >= 0) & (gap <= a1)
    m01 = gap + HALF <= a1
    s00 = jnp.where(m00, scores[:HALF, :HALF], 0.0)
    s11 = jnp.where(m11, scores[HALF:, HALF:], 0.0)
    s01 = jnp.where(m01, scores[:HALF, HALF:], 0.0)
    c2 = cum[...] * LOG2E
    cr = c2 - jnp.log2(softplus(pre[...]))
    c2t = c2.T
    lane = lax.broadcasted_iota(jnp.int32, (HALF, LANES), 1)
    zero = jnp.zeros((HALF, HALF), f32)
    d00, d01, d11 = zero, zero, zero
    cf0, cf1 = zero, zero
    rft[...] = jnp.zeros_like(rft)
    for j in range(val.shape[1] // LANES):
        cols = slice(j * LANES, (j + 1) * LANES)
        v = val[:, cols]
        dy = dssd[:, cols]
        vm = pair_masks(v, v.shape)
        dm = pair_masks(dy, dy.shape)
        tops, bottoms = [], []
        for which in range(2):
            h = 2 * j + which
            col0 = jnp.broadcast_to(cr[:HALF, h : h + 1], (HALF, HALF))
            col1 = jnp.broadcast_to(cr[HALF:, h : h + 1], (HALF, HALF))
            r0 = c2t[h : h + 1, :HALF]
            r1 = c2t[h : h + 1, HALF:]
            e00 = jnp.exp2(jnp.minimum(r0 - col0, 60.0))
            e01 = jnp.exp2(r1 - col0)
            e11 = jnp.exp2(jnp.minimum(r1 - col1, 60.0))
            tops.append((s00 * e00).astype(bf16))
            tops.append((s01 * e01).astype(bf16))
            bottoms.append((s11 * e11).astype(bf16))
            w0 = dot(vm[which][:HALF], dy, 1, 1)
            w1 = dot(vm[which][HALF:], dy[HALF:], 1, 1)
            de00 = w0[:, :HALF] * e00
            de01 = w0[:, HALF:] * e01
            de11 = w1 * e11
            d00 += de00
            d01 += de01
            d11 += de11
            f00 = de00 * s00
            f01 = de01 * s01
            f11 = de11 * s11
            rft[h : h + 1, :HALF] = jnp.sum(f00, axis=0, keepdims=True)
            rft[h : h + 1, HALF:] = jnp.sum(f01 + f11, axis=0, keepdims=True)
            cf0 = jnp.where(lane == h, jnp.sum(f00 + f01, axis=1, keepdims=True), cf0)
            cf1 = jnp.where(lane == h, jnp.sum(f11, axis=1, keepdims=True), cf1)
        dvi[:HALF, cols] = dot(jnp.concatenate(tops, axis=1), jnp.concatenate([dm[0], dm[1]], axis=0))
        dvi[HALF:, cols] = dot(
            jnp.concatenate(bottoms, axis=1), jnp.concatenate([dm[0][HALF:], dm[1][HALF:]], axis=0)
        )
    cflow[:HALF] = cf0
    cflow[HALF:] = cf1
    rflow[...] = rft[...].T
    d00 = split2(jnp.where(m00, d00, 0.0))
    d01 = split2(jnp.where(m01, d01, 0.0))
    d11 = split2(jnp.where(m11, d11, 0.0))
    b0, b1, c0, c1 = bmat[:HALF], bmat[HALF:], cmat[:HALF], cmat[HALF:]
    dbi[:HALF] = dot(d00[0], c0) + dot(d00[1], c0) + dot(d01[0], c1) + dot(d01[1], c1)
    dbi[HALF:] = dot(d11[0], c1) + dot(d11[1], c1)
    dci[:HALF] = dot(d00[0], b0, 0, 0) + dot(d00[1], b0, 0, 0)
    dci[HALF:] = (
        dot(d01[0], b0, 0, 0) + dot(d01[1], b0, 0, 0) + dot(d11[0], b1, 0, 0) + dot(d11[1], b1, 0, 0)
    )


def outer_kernel(
    n, parts, count, tiles, normed, cotx, dgate, nout,
    val_a, val_b, dssd, bmat, cmat, ager, pre_a, pre_b, cum_a, cum_b, tot_a, tot_b, k_a, k_b, ex,
    dvi_a, dbi_a, dci_a, rflow_a, cflow_a, dvi_b, dbi_b, dci_b, rflow_b, cflow_b, own, other, share, zo,
    rft, keep, send, got, far_out, far_in, sems, *scratch
):
    u = pl.program_id(0)
    v = u - 4 * tiles
    states = Exchange(True, n, parts, (tot_a, tot_b), (k_a, k_b), ex, own, other, scratch[5:])
    sums = PairScatter(n, scratch[:5])
    share_rows = zo.shape[0] // n
    across = lax.rem(lax.axis_index("head") + 2, 4)

    def trade(src, dst, sem, head):
        return pltpu.make_async_remote_copy(
            src_ref=src,
            dst_ref=dst,
            send_sem=sems.at[0, sem],
            recv_sem=sems.at[1, sem],
            device_id={"head": head},
            device_id_type=MESH,
        )

    def swap(half, m):
        return trade(send.at[half, m], got.at[half, m], 2 * half + m, states.partner)

    def cross(m):
        return trade(far_out.at[m], far_in.at[m], 4 + m, across)

    def cross_after(m):
        swap(0, m).wait()
        far_out[m] = (keep[0, m] + got[0, m].astype(f32)).astype(bf16)
        cross(m).start()

    @pl.when(u == 0)
    def _():
        meet([states.partner, across], n)
        states.begin()


    @pl.when(u == tiles)
    def _():
        swap(0, 0).start()

    @pl.when(u == 2 * tiles)
    def _():
        swap(0, 1).start()
        cross_after(0)

    @pl.when(u == 3 * tiles)
    def _():
        swap(1, 0).start()
        cross_after(1)

    @pl.when(v == 0)
    def _():
        swap(1, 1).start()
        states.scan()

    part = keep.shape[3]
    rows = pl.ds(pl.multiple_of(lax.rem(u, tiles) * GROUP, GROUP), GROUP)
    for m, (a, b) in enumerate(((normed, dgate), (cotx, nout))):

        @pl.when((v < 0) & (lax.rem(u // tiles, 2) == m))
        def _():
            res = dot(a[...], b[...], 0, 0)
            half = u // (2 * tiles)
            keep[half, m, rows] = res[:, :part]
            send[half, m, rows] = res[:, part:].astype(bf16)

    @pl.when((v >= 0) & (v < count))
    def _():
        pairs_unit(val_a, dssd, bmat, cmat, ager, pre_a, cum_a, dvi_a, dbi_a, dci_a, rflow_a, cflow_a, rft)

    @pl.when(v >= count)
    def _():
        pairs_unit(val_b, dssd, bmat, cmat, ager, pre_b, cum_b, dvi_b, dbi_b, dci_b, rflow_b, cflow_b, rft)

    pl.when(u == 1)(states.combine)

    pl.when(v == 2 * count - 3)(sums.middle)

    @pl.when(v == count - 2)
    def _():
        swap(1, 0).wait()
        cross(0).wait()

        def total(s):
            at = slice(s * share_rows, (s + 1) * share_rows)
            return keep[1, 0, at] + got[1, 0, at].astype(f32) + far_in[0, at].astype(f32)

        sums.start(total)

    @pl.when(v == 2 * count - 1)
    def _():
        states.settle()
        states.close()
        swap(1, 1).wait()
        cross(1).wait()
        zo[...] = (keep[1, 1] + got[1, 1].astype(f32) + far_in[1].astype(f32)).astype(bf16)
        share[...] = sums.finish()


def slope(x):
    sig = sigmoid(x)
    return sig * (1.0 + x * (1.0 - sig))


def conv_back(i, dco, agex, age, ci, taps, dci, tail, head, gw):
    width = ci.shape[1]
    for r in range(0, GROUP, ROWS):
        ages = [agex[r + m : r + m + ROWS] for m in range(4)]
        for j in range(width // LANES):
            cols = slice(j * LANES, (j + 1) * LANES)
            c = ci[r : r + ROWS, cols].astype(f32)
            acc = None
            for m in range(4):
                x = dco[r + m : r + m + ROWS, cols]
                if m:
                    x = jnp.where(ages[m] >= m, x, 0.0)
                term = x * taps[3 - m : 4 - m, cols]
                acc = term if acc is None else acc + term
                gw[8 * (3 - m) : 8 * (3 - m) + 8, cols] += fold8(x * c)
            dci[r : r + ROWS, cols] = acc.astype(bf16)
            if r == GROUP - ROWS:

                @pl.when(i == 0)
                def _():
                    tail[:, cols] = acc[ROWS - 8 :]

    head[...] = dco[0:8]


def start_next(i, dco, agex, gw, gb):
    @pl.when(i == 0)
    def _():
        dco[GROUP : GROUP + 8] = jnp.zeros((8, dco.shape[1]), f32)
        agex[GROUP : GROUP + 8] = jnp.zeros((8, LANES), jnp.int32)
        gw[...] = jnp.zeros_like(gw)
        gb[...] = jnp.zeros_like(gb)

    @pl.when(i > 0)
    def _():
        dco[GROUP : GROUP + 8] = dco[0:8]
        agex[GROUP : GROUP + 8] = agex[0:8]


def back_step(
    half, i, val, dssd, dvi, bmat, co, ci, age, pre, cum, lout, ka, leav, leav_other, lin, kb, arr, arr_other,
    rflow, cflow, dkk, par, tril, ex, red,
    dci, tail, head, draw, gw, gb, galog, gdtb,
    dco, agex, back, omx, vhi, vlo,
):
    width = val.shape[1]
    heads = width // HEAD_DIM
    start_next(i, dco, agex, gw, gb)

    @pl.when(i == 0)
    def _():
        galog[...] = jnp.zeros_like(galog)
        gdtb[...] = jnp.zeros_like(gdtb)

    agex[0:GROUP] = age[...]
    ds = lout[0] + ka[0, 0:1] * arriving_half(leav, leav_other, half)
    dhi, dlo = split2(ds)
    back[...] = dot(bmat[...], dhi) + dot(bmat[...], dlo)
    p = pre[...]
    delta = softplus(p)
    c = cum[...]
    end = c[GROUP - 1 : GROUP]
    age_end = age[GROUP - 1 : GROUP]
    row = lax.broadcasted_iota(jnp.int32, c.shape, 0)
    tail_keep = jnp.where(GROUP - 1 - row <= age_end, jnp.exp(end - c), 0.0)
    omega = tail_keep * delta
    omx[...] = expand(lanes_below(omega, heads), ex[...])
    for r in range(0, GROUP, ROWS):
        rows = slice(r, r + ROWS)
        for j in range(width // LANES):
            cols = slice(j * LANES, (j + 1) * LANES)
            v = val[rows, cols].astype(f32)
            b = back[rows, cols]
            o = omx[rows, cols]
            dval = par[6:7, cols] * dssd[rows, cols].astype(f32) + dvi[rows, cols] + o * b
            vhi[rows, cols], vlo[rows, cols] = split2(v * b)
            d = dval * slope(co[rows, cols])
            dco[rows, cols] = d
            gb[:, cols] += fold8(d)
    domega = dot(vhi[...], red[...]) + dot(vlo[...], red[...])
    flow = domega * omega
    sin = lin[0] + kb[0, 0:1] * arriving_half(arr, arr_other)
    carry = jnp.broadcast_to(jnp.sum(ds * sin, axis=0, keepdims=True), (8, width))
    carry = dot(carry, red[...].astype(f32), precision=HIGHEST)[0:1]
    keep = jnp.where(age_end >= GROUP, jnp.exp(end), 0.0)
    dcum = rflow[...] - cflow[...] + dkk[...] - flow
    ending = jnp.sum(flow, axis=0, keepdims=True) + carry * keep
    dcum = dcum + jnp.where(row == GROUP - 1, ending, 0.0)
    dlog = dot(tril[...], dcum, 0, 0, precision=HIGHEST)
    sig = sigmoid(p)
    ratio = jnp.where(delta > 1e-30, sig / delta, 1.0)
    rate = par[7:8, 0:LANES]
    drf = cflow[...] * ratio + (domega * tail_keep + dlog * rate) * sig
    drf = lanes_below(drf, heads)
    draw[...] = drf.astype(bf16)
    gdtb[...] += fold8(drf)
    galog[...] += fold8(dlog * delta * rate)
    conv_back(i, dco, agex, age, ci, par, dci, tail, head, gw)


def maps_step(
    i, dbi_a, dbi_b, dci_a, dci_b, dcin, co, ci, age, taps,
    val_a, val_b, pre_a, pre_b, cum_a, cum_b, lout_a, lout_b, ka_a, ka_b, leav, leav_other, ex,
    dci, tail, head, gw, gb, dco, agex, dbin,
):
    start_next(i, dco, agex, gw, gb)
    agex[0:GROUP] = age[...]
    age_end = age[GROUP - 1 : GROUP]
    width = val_a.shape[1]
    row = lax.broadcasted_iota(jnp.int32, (GROUP, LANES), 0)
    total = dbi_a[...] + dbi_b[...]
    for half, (val, pre, cum, lout, ka) in enumerate(
        ((val_a, pre_a, cum_a, lout_a, ka_a), (val_b, pre_b, cum_b, lout_b, ka_b))
    ):
        dhi, dlo = split2(lout[0] + ka[0, 0:1] * arriving_half(leav, leav_other, half))
        c = cum[...]
        tail_keep = jnp.where(GROUP - 1 - row <= age_end, jnp.exp(c[GROUP - 1 : GROUP] - c), 0.0)
        omx = expand(lanes_below(tail_keep * softplus(pre[...]), width // HEAD_DIM), ex[...])
        ohi, olo = split2(omx * val[...].astype(f32))
        total = total + dot(ohi, dhi, 1, 1) + dot(ohi, dlo, 1, 1) + dot(olo, dhi, 1, 1)
    dbin[...] = total
    for r in range(0, GROUP, ROWS):
        rows = slice(r, r + ROWS)
        dc = dci_a[rows] + dci_b[rows] + dcin[rows]
        for j, d in enumerate((dbin[rows], dc)):
            cols = slice(j * LANES, (j + 1) * LANES)
            d = d * slope(co[rows, cols])
            dco[rows, cols] = d
            gb[:, cols] += fold8(d)
    conv_back(i, dco, agex, age, ci, taps, dci, tail, head, gw)


def mended(x, last, scr):
    scr[...] = x[...]

    @pl.when(pl.program_id(0) == pl.num_programs(0) - 1)
    def _():
        scr[GROUP - 16 :] = last[...]

    return scr


def padded_rows(x, rows):
    if x.shape[0] == rows:
        return x
    return jnp.concatenate([x, jnp.zeros((rows - x.shape[0], x.shape[1]), x.dtype)], axis=0)


def up16(rows):
    return (rows + 15) // 16 * 16


class Scatter:
    def __init__(self, n, scratch):
        self.n, self.me = n, lax.axis_index("seq")
        self.out, self.got, self.sems = scratch

    @staticmethod
    def scratch(n, rows, cols):
        pad = up16(rows)
        return [
            pltpu.VMEM((n, pad, cols), bf16),
            pltpu.VMEM((n, pad, cols), bf16),
            pltpu.SemaphoreType.DMA((2, n)),
        ]

    def move(self, d):
        to = lax.rem(self.me + d, self.n)
        return pltpu.make_async_remote_copy(
            src_ref=self.out.at[to],
            dst_ref=self.got.at[self.me],
            send_sem=self.sems.at[0, d],
            recv_sem=self.sems.at[1, d],
            device_id={"seq": to},
            device_id_type=MESH,
        )

    def start(self, share):
        for s in range(self.n):
            self.out[s] = padded_rows(share(s), self.out.shape[1]).astype(bf16)
        for d in range(1, self.n):
            self.move(d).start()
        self.got[self.me] = self.out[self.me]

    def finish(self):
        return self.finish_f32().astype(bf16)

    def finish_f32(self):
        for d in range(1, self.n):
            self.move(d).wait()
        total = self.got[0].astype(f32)
        for s in range(1, self.n):
            total = total + self.got[s].astype(f32)
        return total


class Gather:
    def __init__(self, n, scratch):
        self.n, self.me = n, lax.axis_index("seq")
        self.mine, self.all, self.sems = scratch

    @staticmethod
    def scratch(n, rows, cols):
        pad = up16(rows)
        return [
            pltpu.VMEM((pad, cols), bf16),
            pltpu.VMEM((n, pad, cols), bf16),
            pltpu.SemaphoreType.DMA((2, n)),
        ]

    def move(self, d):
        return pltpu.make_async_remote_copy(
            src_ref=self.mine,
            dst_ref=self.all.at[self.me],
            send_sem=self.sems.at[0, d],
            recv_sem=self.sems.at[1, d],
            device_id={"seq": lax.rem(self.me + d, self.n)},
            device_id_type=MESH,
        )

    def start(self, share):
        self.mine[...] = share
        for d in range(1, self.n):
            self.move(d).start()
        self.all[self.me] = share

    def finish(self):
        for d in range(1, self.n):
            self.move(d).wait()

    def rows(self, s, count):
        return self.all[s].astype(f32)[:count]


class PairScatter:
    def __init__(self, n, scratch):
        me = lax.axis_index("seq")
        self.n, self.m, self.odd, self.at = n, n // 2, lax.rem(me, 2), me // 2
        self.partner = me + 1 - 2 * self.odd
        self.out, self.near, self.part, self.got, self.sems = scratch

    @staticmethod
    def scratch(n, rows, cols):
        pad, m = up16(rows), n // 2
        return [
            pltpu.VMEM((2, m, pad, cols), bf16),
            pltpu.VMEM((m, pad, cols), bf16),
            pltpu.VMEM((m, pad, cols), bf16),
            pltpu.VMEM((m, pad, cols), bf16),
            pltpu.SemaphoreType.DMA((2, m)),
        ]

    def move(self, d):
        if d == 0:
            src, dst, to = self.out.at[1 - self.odd], self.near, self.partner
        else:
            to = lax.rem(self.at + d, self.m)
            src, dst, to = self.part.at[to], self.got.at[self.at], 2 * to + self.odd
        return pltpu.make_async_remote_copy(
            src_ref=src,
            dst_ref=dst,
            send_sem=self.sems.at[0, d],
            recv_sem=self.sems.at[1, d],
            device_id={"seq": to},
            device_id_type=MESH,
        )

    def start(self, share):
        for s in range(self.n):
            self.out[s % 2, s // 2] = padded_rows(share(s), self.near.shape[1]).astype(bf16)
        self.move(0).start()

    def middle(self):
        self.move(0).wait()
        for k in range(self.m):
            self.part[k] = (self.out[self.odd, k].astype(f32) + self.near[k].astype(f32)).astype(bf16)
        for d in range(1, self.m):
            self.move(d).start()
        self.got[self.at] = self.part[self.at]

    def finish(self):
        for d in range(1, self.m):
            self.move(d).wait()
        total = self.got[0].astype(f32)
        for k in range(1, self.m):
            total = total + self.got[k].astype(f32)
        return total.astype(bf16)


class PairGather:
    def __init__(self, n, scratch):
        me = lax.axis_index("seq")
        self.n, self.m, self.odd, self.at = n, n // 2, lax.rem(me, 2), me // 2
        self.partner = me + 1 - 2 * self.odd
        self.mine, self.all, self.sems = scratch

    @staticmethod
    def scratch(n, rows, cols):
        pad, m = up16(rows), n // 2
        return [
            pltpu.VMEM((pad, cols), bf16),
            pltpu.VMEM((2, m, pad, cols), bf16),
            pltpu.SemaphoreType.DMA((2, m)),
        ]

    def move(self, d):
        if d == 0:
            src, dst, to = self.all.at[self.odd], self.all.at[self.odd], self.partner
        else:
            src, dst = self.mine, self.all.at[self.odd, self.at]
            to = 2 * lax.rem(self.at + d, self.m) + self.odd
        return pltpu.make_async_remote_copy(
            src_ref=src,
            dst_ref=dst,
            send_sem=self.sems.at[0, d],
            recv_sem=self.sems.at[1, d],
            device_id={"seq": to},
            device_id_type=MESH,
        )

    def start(self, share):
        self.mine[...] = share
        for d in range(1, self.m):
            self.move(d).start()
        self.all[self.odd, self.at] = share

    def middle(self):
        for d in range(1, self.m):
            self.move(d).wait()
        self.move(0).start()

    def finish(self):
        self.move(0).wait()

    def rows(self, s, count):
        return self.all[s % 2, s // 2].astype(f32)[:count]


def mend(got, tail, ci, next_age, taps, dx, scr, last, flip):
    g = got[...]
    if flip:
        part = g.shape[1] // 2
        g = jnp.concatenate([g[:, part:], g[:, :part]], axis=1)
    rows = scr.shape[0]
    if dx is not None:
        scr[...] = dx[...]
    ending = ci[...].astype(f32)[8:16]
    row = lax.broadcasted_iota(jnp.int32, (8, LANES), 0)
    fixed, sums = [], []
    for j in range(g.shape[1] // LANES):
        cols = slice(j * LANES, (j + 1) * LANES)
        acc = tail[:, cols]
        parts = [jnp.zeros((1, LANES), f32)] * 4
        for m in range(1, 4):
            use = (row >= 8 - m) & (pltpu.roll(next_age[...], 8 - m, 0) >= m)
            x = jnp.where(use, pltpu.roll(g[:, cols], 8 - m, 0), 0.0)
            acc = acc + x * taps[3 - m : 4 - m, cols]
            parts[3 - m] = jnp.sum(x * ending[:, cols], axis=0, keepdims=True)
        fixed.append(acc)
        sums.append(jnp.concatenate(parts, axis=0))
    fixed = jnp.concatenate(fixed, axis=1)
    before = scr[rows - 16 :].astype(f32)[0:8]
    scr[rows - 16 :] = jnp.concatenate([before, fixed], axis=0).astype(bf16)
    if last is not None:
        last[...] = scr[rows - 16 :]
    return jnp.concatenate(sums, axis=1)


def small_sums(at, fix, gw, gb, galog, gdtb, gskip, ggain, red, small_keep, small_send):
    part = red.shape[0] // 2
    heads = part // HEAD_DIM
    width = 2 * part
    for to in (small_keep, small_send):
        to[...] = jnp.zeros_like(to)
    taps = [jnp.sum(gw[8 * k : 8 * k + 8], axis=0, keepdims=True) for k in range(4)]
    taps = jnp.concatenate(taps, axis=0) + fix
    bias = jnp.sum(gb[...], axis=0, keepdims=True)
    cols = slice(at * width, (at + 1) * width)
    gain = jnp.sum(ggain[:, cols], axis=0, keepdims=True)
    skip = jnp.broadcast_to(jnp.sum(gskip[:, cols], axis=0, keepdims=True), (8, width))
    skip = dot(skip, red[...].astype(f32), precision=HIGHEST)
    step = jnp.broadcast_to(jnp.sum(gdtb[...], axis=0, keepdims=True), (8, LANES))
    log = jnp.broadcast_to(jnp.sum(galog[...], axis=0, keepdims=True), (8, LANES))
    for k, to in enumerate((small_keep, small_send)):
        mine = slice(k * part, (k + 1) * part)
        to[0:4, 0:part] = taps[:, mine]
        to[4:5, 0:part] = bias[:, mine]
        to[5:6, 0:part] = gain[:, mine]
        row = jnp.zeros((8, LANES), f32)
        for place, x in enumerate((step, log, skip)):
            x = lanes_below(pltpu.roll(x, (LANES - k * heads) % LANES, 1), heads)
            row = row + pltpu.roll(x, place * heads, 1)
        to[6:7, 0:LANES] = row[0:1]


def half_tile(tile, normed, dx, draw, keep, send, small_keep, small_send):
    part = keep.shape[1]
    heads = part // HEAD_DIM
    res = dot(normed[...], dx[...], 0, 0)
    keep[...] = res[:, :part]
    send[...] = res[:, part:].astype(bf16)
    dt = dot(draw[...], normed[...], 0, 0)
    cols = pl.ds(pl.multiple_of(tile * GROUP, GROUP), GROUP)
    small_keep[8:16, cols] = dt[0:8]
    small_send[8:16, cols] = pltpu.roll(dt, LANES - heads, 0)[0:8]


def turn_kernel(n, parts, count, *refs):
    maps_in, refs = refs[:22], refs[22:]
    back_in, refs = refs[:24], refs[24:]
    (own, share, pieces), refs = refs[:3], refs[3:]
    maps_out, refs = refs[:5], refs[5:]
    back_out, refs = refs[:8], refs[8:]
    (share_out, gathered, placed), refs = refs[:3], refs[3:]
    maps_scr, refs = refs[:3], refs[3:]
    back_scr, refs = refs[:6], refs[6:]
    (piece_sems,), refs = refs[:1], refs[1:]
    u = pl.program_id(0)
    sums, shares = PairScatter(n, refs[:5]), PairGather(n, refs[5:])
    rows = own.shape[0] // n
    me = lax.axis_index("seq")
    head = lax.axis_index("head")
    near = head + 1 - 2 * lax.rem(head, 2)
    heads = [head, near, lax.rem(head + 2, 4), lax.rem(near + 2, 4)]
    chunk = pieces.shape[2]

    def piece_copy(k):
        cols = pl.ds(pl.multiple_of(lax.rem(head, parts) * chunk, chunk), chunk)
        src, dst = pieces.at[heads[k]], placed.at[head // parts, :, cols]
        if k == 0:
            return pltpu.make_async_copy(src, dst, piece_sems.at[0, 0])
        return pltpu.make_async_remote_copy(
            src_ref=src,
            dst_ref=dst,
            send_sem=piece_sems.at[0, k],
            recv_sem=piece_sems.at[1, k],
            device_id={"head": heads[k]},
            device_id_type=MESH,
        )

    @pl.when(u == 0)
    def _():
        barrier = pltpu.get_barrier_semaphore()
        for k in range(1, 4):
            pl.semaphore_signal(barrier, inc=1, device_id={"head": heads[k]}, device_id_type=MESH)
        for d in range(1, n):
            pl.semaphore_signal(barrier, inc=1, device_id={"seq": lax.rem(me + d, n)}, device_id_type=MESH)
        pl.semaphore_wait(barrier, n + 2)
        shares.start(share[...])
        sums.start(lambda s: own[s * rows : (s + 1) * rows].astype(f32))
        for k in (2, 3, 1, 0):
            piece_copy(k).start()

    @pl.when(u < count)
    def _():
        maps_step(u, *maps_in, *maps_out, *maps_scr)

    @pl.when(u >= count)
    def _():
        back_step(1, u - count, *back_in, *back_out, *back_scr)

    @pl.when(u == count - 1)
    def _():
        sums.middle()
        shares.middle()

    @pl.when(u == 2 * count - 1)
    def _():
        share_out[...] = sums.finish()
        shares.finish()
        for s in range(n):
            gathered[s * rows : (s + 1) * rows] = shares.rows(s, rows)
        for k in range(4):
            piece_copy(k).wait()


def late_kernel(n, parts, count, tiles, *refs):
    back_in, refs = refs[:24], refs[24:]
    (
        normed, dx_b, tail_b, head_b, ci_b, par_b, draw_b, gw_b, gb_b, galog_b, gdtb_b,
        dbc, tail_bc, head_bc, ci_bc, taps_bc, gw_bc, gb_bc, ci_a, next_age, gskip, ggain_out, share,
    ), refs = refs[:23], refs[23:]
    (hid, cotx, gain, dgate, z0, z1, z2, z3, bcw, x0, x1, x2, x3, dt_a, dt_b), refs = refs[:15], refs[15:]
    (grad_in, gx, gbc, small, grad_out), refs = refs[:5], refs[5:]
    back_scr, refs = refs[:6], refs[6:]
    (
        dx_a, draw_a, keep_a, send_a, small_a, small_send_a, got_a, small_got_a, last,
        tail_a, head_a, gw_a, gb_a, galog_a, gdtb_a, scr_b, scr_bc, keep_b, send_b, got_b, far_out,
        small_b, small_send_b, small_got, small_out, small_in, far_in, edge_b, edge_bc, edge_a,
        g_bc, bc_out, bc_got, bc_far_out, bc_far, bc_own, small_bc, com_got, bc_heads,
        acc_s, low, shuffle, landed, ggain, gi_got, gi_sum, edge_sems, sems, piece_sems,
    ), refs = refs[:49], refs[49:]
    u = pl.program_id(0)
    par_a, red = back_in[20], back_in[23]
    s_me = lax.axis_index("seq")
    heads = head_peers()
    h_me, near, across = heads[:3]
    half = lax.rem(h_me, parts)
    to_seq = s_me - 1 + half
    has_before = to_seq >= 0
    has_after = s_me + half < n
    chunk = count * GROUP
    part = keep_a.shape[1]
    features = gain.shape[1]
    lane_tiles = features // LANES
    first_bc, first_b, first_back, first_a = 1, tiles + 1, 2 * tiles + 1, 2 * tiles + count
    first_out = first_a + tiles
    pack_rows = -(-24 // n)
    pack = up16(4 * pack_rows + 4)
    bc_rows = features // 4
    share_rows = bc_rows // n
    gathered, gx_sum, gx_all = PairGather(n, refs[:3]), Scatter(n, refs[3:6]), Gather(n, refs[6:9])
    bc_sum, bc_all = Scatter(n, refs[9:12]), Gather(n, refs[12:15])

    def trade(src, dst, sem, head):
        return send(src, dst, sems, sem, {"head": head})

    def edge(k):
        src, dst = ((head_b, edge_b), (head_bc, edge_bc), (head_a, edge_a))[k]
        return send(src, dst, edge_sems, k, {"seq": lax.max(to_seq, 0), "head": near})

    def send_edge(k):
        pl.when(has_before)(edge(k).start)

    def take_edge(k):
        pl.when(has_before)(edge(k).wait_send)
        pl.when(has_after)(edge(k).wait_recv)

    swap_b = trade(send_b, got_b, 0, near)
    swap_small = trade(small_send_b, small_got, 1, near)
    cross_b = trade(far_out, far_in, 2, across)
    cross_small = trade(small_out, small_in, 3, across)
    swap_a = trade(send_a, got_a, 4, near)
    swap_small_a = trade(small_send_a, small_got_a, 5, near)

    swap_bc = trade(bc_out, bc_got, 6, near)
    cross_bc = trade(bc_far_out, bc_far, 7, across)

    def bc_quarter(k):
        return g_bc[pl.ds(pl.multiple_of(heads[k] * bc_rows, 8), bc_rows)]

    def common_trade(k):
        return trade(small_bc, com_got.at[k], 8 + k, heads[k])

    def heads_trade(k):
        return trade(bc_all.all, bc_heads.at[h_me], 11 + k, heads[k])

    def gi_trade(k):
        return trade(gi_sum, gi_got.at[k], 14 + k, heads[k])

    def piece_copy(step, k):
        return pltpu.make_async_remote_copy(
            src_ref=shuffle.at[step, heads[k]],
            dst_ref=landed.at[step, k],
            send_sem=piece_sems.at[0, step, k],
            recv_sem=piece_sems.at[1, step, k],
            device_id={"head": heads[k]},
            device_id_type=MESH,
        )

    def place(step, k):
        cols = pl.ds(pl.multiple_of(lax.rem(heads[k], parts) * chunk + step * GROUP, GROUP), GROUP)
        grad_in[heads[k] // parts, :, cols] = landed[step, k] if k else shuffle[step, h_me]

    @pl.when(u == 0)
    def _():
        for to in (edge_b, edge_bc, edge_a, ggain, gi_sum):
            to[...] = jnp.zeros_like(to)
        barrier = pltpu.get_barrier_semaphore()
        for head in heads[1:]:
            pl.semaphore_signal(barrier, inc=1, device_id={"head": head}, device_id_type=MESH)
        for d in range(1, n):
            pl.semaphore_signal(barrier, inc=1, device_id={"seq": lax.rem(s_me + d, n)}, device_id_type=MESH)
        other_seq = s_me - 1 + 2 * half
        has_other = (other_seq >= 0) & (other_seq < n)

        @pl.when(has_other)
        def _():
            pl.semaphore_signal(
                barrier, inc=1, device_id={"seq": other_seq, "head": near}, device_id_type=MESH
            )

        pl.semaphore_wait(barrier, n + 2 + has_other.astype(jnp.int32))
        send_edge(0)
        send_edge(1)
        gathered.start(share[...])

    block = jnp.clip(u - 2 * tiles, 0, count - 1)

    @pl.when((u == 0) | ((u >= first_back) & (u < first_a)))
    def _():
        rows = pl.ds(pl.multiple_of((count - 1 - block) * GROUP, GROUP), GROUP)
        outs = (dx_a.at[rows], tail_a, head_a, draw_a.at[rows], gw_a, gb_a, galog_a, gdtb_a)
        back_step(0, block, *back_in, *outs, *back_scr)

    @pl.when(u == first_bc)
    def _():
        take_edge(1)
        fix = mend(edge_bc, tail_bc, ci_bc, next_age, taps_bc, dbc, scr_bc, None, False)
        small_bc[...] = jnp.zeros_like(small_bc)
        sums = [jnp.sum(gw_bc[8 * k : 8 * k + 8], axis=0, keepdims=True) for k in range(4)]
        small_bc[0:4] = jnp.concatenate(sums, axis=0) + fix
        small_bc[4:5] = jnp.sum(gb_bc[...], axis=0, keepdims=True)
        for k in range(1, 4):
            common_trade(k).start()

    @pl.when((u >= first_bc) & (u < first_b))
    def _():
        rows = pl.ds(pl.multiple_of((u - first_bc) * GROUP, GROUP), GROUP)
        g_bc[rows] = dot(normed[...], scr_bc[...], 0, 0)

    @pl.when(u == first_b)
    def _():
        bc_out[0] = bc_quarter(1).astype(bf16)
        bc_out[1] = bc_quarter(3).astype(bf16)
        swap_bc.start()
        take_edge(0)
        fix = mend(edge_b, tail_b, ci_b, next_age, par_b, dx_b, scr_b, None, True)
        small_sums(1, fix, gw_b, gb_b, galog_b, gdtb_b, gskip, ggain_out, red, small_b, small_send_b)

    @pl.when(u == first_b + 1)
    def _():
        swap_bc.wait()
        bc_far_out[...] = (bc_quarter(2) + bc_got[1].astype(f32)).astype(bf16)
        cross_bc.start()
        gathered.middle()

    @pl.when((u >= first_b) & (u < first_back))
    def _():
        rows = pl.ds(pl.multiple_of((u - first_b) * GROUP, GROUP), GROUP)
        half_tile(u - first_b, normed, scr_b, draw_b, keep_b.at[rows], send_b.at[rows], small_b, small_send_b)

    @pl.when(u == first_back)
    def _():
        swap_b.start()
        swap_small.start()
        cross_bc.wait()
        bc_own[...] = bc_quarter(0) + bc_got[0].astype(f32) + bc_far[...].astype(f32)
        bc_sum.start(lambda s: bc_own[s * share_rows : (s + 1) * share_rows])

    @pl.when(u == first_back + 1)
    def _():
        swap_b.wait()
        far_out[...] = (keep_b[...] + got_b[...].astype(f32)).astype(bf16)
        cross_b.start()
        swap_small.wait()
        small_out[...] = small_b[...] + small_got[...]
        cross_small.start()
        bc_all.start(bc_sum.finish())

    @pl.when(u == first_back + 2)
    def _():
        bc_all.finish()
        for k in range(1, 4):
            heads_trade(k).start()
        bc_heads[h_me] = bc_all.all[...]

    @pl.when(u == first_a)
    def _():
        send_edge(2)
        gathered.finish()
        rows = grad_out.shape[1] // n
        grad_out[...] = jnp.concatenate([gathered.rows(s, rows) for s in range(n)], axis=0).T
        take_edge(2)
        fix = mend(edge_a, tail_a, ci_a, next_age, par_a, None, dx_a, None, True)
        small_sums(0, fix, gw_a, gb_a, galog_a, gdtb_a, gskip, ggain_out, red, small_a, small_send_a)

    @pl.when((u >= first_a) & (u < first_out))
    def _():
        rows = pl.ds(pl.multiple_of((u - first_a) * GROUP, GROUP), GROUP)
        half_tile(u - first_a, normed, dx_a, draw_a, keep_a.at[rows], send_a.at[rows], small_a, small_send_a)

    def halves_of(x):
        x = jnp.concatenate([x[:, :part], x[:, part:]], axis=0)
        hi = x.astype(bf16).astype(f32)
        return jnp.concatenate([hi, x - hi], axis=0)

    def joined(x, rows):
        x = x[0 : 2 * rows] + x[2 * rows : 4 * rows]
        return jnp.concatenate([x[:rows], x[rows:]], axis=1)

    @pl.when(u == first_out - 1)
    def _():
        swap_a.start()
        swap_small_a.start()

    @pl.when(u == first_out)
    def _():
        cross_small.wait()
        both = small_bc[...]
        for k in range(1, 4):
            common_trade(k).wait()
            both = both + com_got[k]
        both = jnp.concatenate([both, jnp.zeros((8, features - 2 * LANES), f32)], axis=1)
        cross_b.wait()
        swap_small_a.wait()
        both = jnp.concatenate([small_a[...] + small_got_a[...] + small_in[...], both], axis=0)
        swap_a.wait()
        rows = features // n

        def gx_share(s):
            at = slice(s * rows, (s + 1) * rows)
            x = keep_a[at] + got_a[at].astype(f32) + far_in[at].astype(f32)
            if s * pack_rows < 24:
                x = jnp.concatenate([x, halves_of(both[s * pack_rows : (s + 1) * pack_rows])], axis=0)
            return x

        gx_sum.start(gx_share)

    @pl.when(u >= first_out)
    def _():
        step = u - first_out
        at = pl.ds(pl.multiple_of(step * GROUP, GROUP), GROUP)
        acc = dot(scr_bc[at], bcw[...], 1, 1) + dot(draw_a[at], dt_a[...]) + dot(draw_b[at], dt_b[...])
        for k, (z, x) in enumerate(((z0, x0), (z1, x1), (z2, x2), (z3, x3))):
            d, col = (dx_a if k < 2 else scr_b), (k % 2) * part
            acc = acc + dot(dgate[:, k * part : (k + 1) * part], z[...], 1, 1)
            acc = acc + dot(d[at, col : col + part], x[...], 1, 1)
        acc_s[...] = acc
        piece = features // 4
        for r in range(0, GROUP, ROWS):
            rows = slice(r, r + ROWS)
            x = hid[rows].astype(f32)
            rinv = lax.rsqrt(jnp.sum(x * x, axis=1, keepdims=True) / x.shape[1] + EPS)
            xhat = x * rinv
            d = acc_s[rows]
            ggain[...] += fold8(d * xhat)
            dxh = d * gain[0:1]
            mean = jnp.sum(dxh * xhat, axis=1, keepdims=True) / x.shape[1]
            low[rows] = (cotx[rows].astype(f32) + rinv * (dxh - xhat * mean)).astype(bf16)
        turned = low[...].T
        for k in range(4):
            shuffle[step, k] = turned[k * piece : (k + 1) * piece]
        for k in (2, 3, 1):
            piece_copy(step, k).start()

    @pl.when(u == first_out + count - 1)
    def _():
        rows = features // n
        small_at = rows + 4 * pack_rows
        total = gx_sum.finish_f32()
        sums = halves_of(joined(total[rows:], pack_rows))
        row = halves_of(jnp.sum(ggain[...], axis=0, keepdims=True))
        gx_all.start(padded_rows(jnp.concatenate([total[:rows], sums, row], axis=0), total.shape[0]).astype(bf16))
        for k in range(1, 4):
            heads_trade(k).wait()
        for q in range(4):
            for s in range(n):
                at = (q * n + s) * share_rows
                gbc[at : at + share_rows] = bc_heads[q, s].astype(f32)[:share_rows]
        for step in range(count):
            for k in range(4):
                if k:
                    piece_copy(step, k).wait()
                place(step, k)
        gx_all.finish()
        row = joined(gx_all.rows(0, small_at + 4)[small_at:], 1)
        for s in range(1, n):
            row = row + joined(gx_all.rows(s, small_at + 4)[small_at:], 1)
        for t in range(lane_tiles):
            gi_sum[t : t + 1] = row[:, t * LANES : (t + 1) * LANES]
        for k in range(1, 4):
            gi_trade(k).start()
        for s in range(n):
            share_s = gx_all.rows(s, small_at)
            gx[s * rows : (s + 1) * rows] = share_s[:rows]
            if s * pack_rows < 24:
                small[s * pack_rows : (s + 1) * pack_rows] = joined(share_s[rows:], pack_rows)
        total = gi_sum[...]
        for k in range(1, 4):
            gi_trade(k).wait()
            total = total + gi_got[k]
        for t in range(lane_tiles):
            small[24:32, t * LANES : (t + 1) * LANES] = jnp.broadcast_to(total[t : t + 1], (8, LANES))


def unpack_kernel(
    quarter, heads, me, small, gi, dt, taps, bias, maps, maps_bias, step, log, skip, gain
):
    features = small.shape[1]
    piece = gi.shape[1]
    row = pltpu.roll(small[24:32], lax.rem(features - me[0] * piece, features), 1)
    gi[...] = row[0:1, :piece]
    dt[...] = small[8 : 8 + heads]
    taps[...] = small[0:4, :quarter]
    bias[...] = small[4:5, :quarter]
    gain[...] = small[5:6, :quarter]
    maps[...] = small[16:20, : 2 * LANES]
    maps_bias[...] = small[20:21, : 2 * LANES]
    row = jnp.broadcast_to(small[6:7, 0:LANES], (8, LANES))
    for k, to in enumerate((step, log, skip)):
        to[...] = pltpu.roll(row, LANES - k * heads, 1)[0:1, :heads] if k else row[0:1, :heads]


def shards(
    hidden_in,
    output_cotangent,
    input_norm_scale_gain,
    z_proj,
    x_proj,
    bc_proj,
    dt_proj,
    conv_x_weight,
    conv_x_bias,
    conv_bc_weight,
    conv_bc_bias,
    dt_bias,
    a_log,
    d_skip,
    out_norm_gain,
    out_proj,
    doc_starts,
):
    batch, tokens, features = hidden_in.shape
    quarter = z_proj.shape[1]
    width = 2 * quarter
    inner = 4 * quarter
    heads = dt_proj.shape[1]
    seqs = lax.axis_size("seq")
    head_devices = lax.axis_size("head")
    parts = head_devices // batch
    chunk = tokens // parts
    count = chunk // GROUP
    si, hi_ = lax.axis_index("seq"), lax.axis_index("head")
    seq_of, half = hi_ // parts, hi_ % parts
    meta = jnp.reshape(hi_, (1,)).astype(jnp.int32)

    here = lambda i, *_: (i, 0)
    here3 = lambda i, *_: (i, 0, 0)
    rev = lambda i, *_: (count - 1 - i, 0)
    rev3 = lambda i, *_: (count - 1 - i, 0, 0)
    rev_hid = lambda i, m: (m[0] // parts, lax.rem(m[0], parts) * count + count - 1 - i, 0)
    taps_bc = conv_bc_weight.T
    lane_block = (GROUP, LANES)
    map_block = (GROUP, 2 * LANES)
    wide = (GROUP, inner)
    half_in = (GROUP, width)
    state_block = (1, LANES, width)
    keep_block = (1, 8, width)
    piece = features // head_devices
    ex, red = expansion(width)
    tril = jnp.asarray(np.tril(np.ones((GROUP, GROUP), np.float32)))
    cotangent = jnp.swapaxes(output_cotangent, 1, 2)

    def whole(*arrays):
        return [(a, None, None) for a in arrays]

    vecs = jnp.concatenate(
        [
            conv_x_bias,
            out_norm_gain,
            jnp.pad(jnp.concatenate([dt_bias, a_log, d_skip]), (0, 2 * LANES - 3 * heads)),
            input_norm_scale_gain,
            conv_bc_bias,
        ]
    ).reshape(-1, LANES)
    front_scratch = [
        pltpu.VMEM((GROUP + 8, width), f32),
        pltpu.VMEM((LANES, width), f32),
        pltpu.VMEM((8, LANES), f32),
        pltpu.VMEM(half_in, f32),
        pltpu.VMEM(half_in, bf16),
        pltpu.VMEM(half_in, bf16),
        pltpu.VMEM((LANES, features), f32),
        pltpu.VMEM((GROUP + 8, 2 * LANES), f32),
    ]

    def front_outs(block, block3):
        return [
            ((chunk, width), bf16, half_in, block),
            ((chunk, width), f32, half_in, block),
            ((chunk, width), bf16, half_in, block),
            ((chunk, LANES), f32, lane_block, block),
            ((chunk, LANES), f32, lane_block, block),
            ((count, LANES, width), f32, state_block, block3),
            ((count, 8, width), f32, keep_block, block3),
            ((count, 8, width), f32, keep_block, block3),
            ((LANES, width), f32, None, None),
            ((8, LANES), f32, None, None),
            ((8, width), f32, None, None),
            ((LANES, features), bf16, None, None),
        ]

    own_head = lambda: lax.axis_index("head")
    x_shape = (features, quarter)

    def phase(k, rank):
        at = lambda u: jnp.clip(u - k * count, 0, count - 1)
        return (lambda u: (at(u), 0)) if rank == 2 else (lambda u: (at(u), 0, 0))

    def front_outs(k):
        return [
            ((chunk, width), bf16, half_in, phase(k, 2)),
            ((chunk, width), f32, half_in, phase(k, 2)),
            ((chunk, width), bf16, None, None),
            ((chunk, LANES), f32, None, None),
            ((chunk, LANES), f32, None, None),
            ((count, LANES, width), f32, state_block, phase(k, 3)),
            ((count, 8, width), f32, keep_block, phase(k, 3)),
            ((count, 8, width), f32, keep_block, phase(k, 3)),
            ((8, width), f32, None, None),
            ((LANES, features), bf16, None, None),
            ((LANES, quarter), f32, None, None),
            ((LANES, quarter), f32, None, None),
            ((chunk, width), f32, half_in, phase(k + 2, 2)),
        ]

    front_names = ("ci", "co", "val", "pre", "cum", "lin", "kb", "ck", "par", "dtp", "own", "other", "part")
    outs = run(
        functools.partial(forward_kernel, seqs, parts, count),
        (5 * count,),
        [
            (
                hidden_in,
                (1, GROUP, features),
                lambda u: (own_head() // parts, lax.rem(own_head(), parts) * count + jnp.minimum(u, count - 1), 0),
            ),
            (hidden_in, (1, 16, features), lambda u: (own_head() // parts, tokens // 16 - 1, 0)),
            (hidden_in, (1, 16, features), lambda u: (own_head() // parts, chunk // 16 - 1, 0)),
            *whole(doc_starts, vecs, conv_x_weight.T, dt_proj.T, x_proj, z_proj, out_proj, bc_proj, taps_bc, tril, ex),
            (cotangent, pl.ANY, None),
        ],
        [
            ((chunk, features), bf16, None, None),
            ((chunk, 2 * LANES), bf16, None, None),
            ((chunk, LANES), jnp.int32, None, None),
            ((8, chunk), jnp.int32, (8, GROUP), lambda u: (0, jnp.minimum(u, count - 1))),
            ((8, LANES), jnp.int32, None, None),
            ((8, features), f32, None, None),
        ]
        + [(x_shape, bf16, None, None)] * 6
        + [((quarter, features), bf16, None, None)] * 3
        + [((piece, chunk), bf16, pl.ANY, None)] * 3
        + [
            ((chunk, 2 * LANES), f32, map_block, phase(1, 2)),
            ((chunk, LANES), bf16, None, None),
            ((chunk, LANES), bf16, None, None),
        ]
        + front_outs(1)
        + front_outs(2),
        [
            pltpu.VMEM((8, features), f32),
            pltpu.VMEM((8, 2 * LANES), f32),
            pltpu.VMEM((16, features), bf16),
            pltpu.VMEM((16, features), bf16),
        ]
        + [pltpu.VMEM((16, features), f32)] * 4
        + [pltpu.VMEM(x_shape, bf16)] * 3
        + [pltpu.VMEM((LANES, width), f32)] * 2
        + [pltpu.VMEM((8, LANES), f32)] * 2
        + [pltpu.SemaphoreType.DMA((2, 7)), pltpu.SemaphoreType.DMA((2, 4))]
        + front_scratch
        + Weights.scratch(features, quarter)
        + Weights.scratch(quarter, features)
        + Exchange.scratch(seqs, quarter) * 2,
        flops=40_000_000_000,
        moved=50_000_000,
        collective=1,
    )
    normed, ci_bc, age, ager, next_age, gain_in = outs[:6]
    xs, zs, os_ = [x_proj, *outs[6:9]], [z_proj, *outs[9:12]], [out_proj, *outs[12:15]]
    cots = outs[15:18]
    co_bc, bmat, cmat = outs[18:21]
    ha, hb = dict(zip(front_names, outs[21:34])), dict(zip(front_names, outs[34:47]))
    halves = [ha, hb]
    for d in halves:
        d["arr"] = [d["own"], d["other"]]

    outs = run(
        mid_kernel,
        (count,),
        [
            (hidden_in, (1, GROUP, features), rev_hid),
            (normed, (GROUP, features), rev),
            *whole(*zs, *os_),
            (
                cotangent,
                (1, piece, GROUP),
                lambda i, m: (m[0] // parts, 0, lax.rem(m[0], parts) * count + count - 1 - i),
            ),
            *[(c, (piece, GROUP), lambda i, *_: (0, count - 1 - i)) for c in cots],
            (cmat, lane_block, rev),
            (age, lane_block, rev),
            *whole(ex, red, ha["par"], hb["par"]),
            *[(d["part"], half_in, rev) for d in halves],
            *[(d["val"], half_in, rev) for d in halves],
            *[(d["cum"], lane_block, rev) for d in halves],
            *[(d["lin"], state_block, rev3) for d in halves],
            *[(d["kb"], keep_block, rev3) for d in halves],
            *[(d["ck"], keep_block, rev3) for d in halves],
            *whole(*ha["arr"], *hb["arr"]),
        ],
        [
            ((4, piece, chunk), bf16, (4, piece, GROUP), lambda i, *_: (0, 0, count - 1 - i)),
            ((chunk, features), bf16, (GROUP, features), rev),
            ((chunk, inner), bf16, wide, rev),
            ((chunk, features), bf16, (GROUP, features), rev),
            ((chunk, inner), bf16, wide, rev),
            ((chunk, inner), bf16, wide, rev),
            ((chunk, LANES), f32, lane_block, rev),
            ((chunk, LANES), f32, lane_block, rev),
            ((chunk, LANES), f32, lane_block, rev),
            ((count, LANES, width), f32, state_block, rev3),
            ((count, LANES, width), f32, state_block, rev3),
            ((count, 8, width), f32, keep_block, rev3),
            ((count, 8, width), f32, keep_block, rev3),
            ((LANES, width), f32, None, None),
            ((LANES, width), f32, None, None),
            ((8, LANES), f32, None, None),
            ((8, LANES), f32, None, None),
            ((8, inner), f32, None, None),
            ((8, inner), f32, None, None),
        ],
        [pltpu.VMEM(wide, f32)] * 6
        + [pltpu.VMEM(wide, bf16)] * 4
        + [pltpu.VMEM((LANES, width), f32)] * 2
        + [pltpu.VMEM((8, LANES), f32)] * 2
        + [pltpu.VMEM((4, piece, GROUP), bf16)],
        flops=30_000_000_000,
        moved=50_000_000,
        prefetch=(meta,),
    )
    pieces, hidc, outs = outs[0], outs[1], outs[2:]
    nout, cotx, dssd, dgate, dcin, ha["dkk"], hb["dkk"], ha["lout"], hb["lout"], ha["ka"], hb["ka"] = outs[:11]
    dtot_a, dtot_b, dk_a, dk_b, ggain_out, gskip = outs[11:]

    tiles = features // GROUP
    lead = 4 * tiles
    tile_block = lambda u: (0, lax.rem(jnp.minimum(u, lead - 1), tiles))
    first_half = lambda u: (0, 1 - jnp.minimum(u // (2 * tiles), 1))
    after_lead = lambda u: jnp.maximum(u - lead, 0)
    lo_unit = lambda u: (jnp.clip(u - lead, 0, count - 1), 0)
    hi_unit = lambda u: (jnp.clip(u - lead - count, 0, count - 1), 0)
    any_unit = lambda u: (lax.rem(after_lead(u), count), 0)
    quarter_grad = (2, features, quarter)
    share_rows = features // seqs
    outs = run(
        functools.partial(outer_kernel, seqs, parts, count, tiles),
        (lead + 2 * count,),
        [
            (normed, (chunk, GROUP), tile_block),
            (cotx, (chunk, GROUP), tile_block),
            (dgate, (chunk, width), first_half),
            (nout, (chunk, width), first_half),
            (ha["val"], half_in, lo_unit),
            (hb["val"], half_in, hi_unit),
            (dssd, half_in, lambda u: (lax.rem(after_lead(u), count), after_lead(u) // count)),
            (bmat, lane_block, any_unit),
            (cmat, lane_block, any_unit),
            (ager, (8, GROUP), lambda u: (0, lax.rem(after_lead(u), count))),
            (ha["pre"], lane_block, lo_unit),
            (hb["pre"], lane_block, hi_unit),
            (ha["cum"], lane_block, lo_unit),
            (hb["cum"], lane_block, hi_unit),
            *whole(dtot_a, dtot_b, dk_a, dk_b, ex),
        ],
        [
            (shape, f32, (GROUP, shape[1]), imap)
            for imap in (lo_unit, hi_unit)
            for shape in [(chunk, width)] + [(chunk, LANES)] * 4
        ]
        + [((LANES, width), f32, None, None)] * 2
        + [((up16(share_rows), quarter), bf16, None, None), ((features, quarter), bf16, None, None)],
        [
            pltpu.VMEM((LANES, GROUP), f32),
            pltpu.VMEM((2,) + quarter_grad, f32),
            pltpu.VMEM((2,) + quarter_grad, bf16),
            pltpu.VMEM((2,) + quarter_grad, bf16),
            pltpu.VMEM(quarter_grad, bf16),
            pltpu.VMEM(quarter_grad, bf16),
            pltpu.SemaphoreType.DMA((2, 6)),
        ]
        + PairScatter.scratch(seqs, share_rows, quarter)
        + Exchange.scratch(seqs, width),
        flops=30_000_000_000,
        moved=40_000_000,
        collective=2,
    )
    names = ("dvi", "dbi", "dci_c", "rflow", "cflow")
    ha.update(zip(names, outs[:5]))
    hb.update(zip(names, outs[5:10]))
    leav = outs[10:12]
    share_z, grad_o = outs[12:]

    def back_ins(n, block, block3):
        d = halves[n]
        return [
            (d["val"], half_in, block),
            (dssd, half_in, lambda u: (block(u)[0], n)),
            (d["dvi"], half_in, block),
            (bmat, lane_block, block),
            (d["co"], half_in, block),
            (d["ci"], half_in, block),
            (age, lane_block, block),
            (d["pre"], lane_block, block),
            (d["cum"], lane_block, block),
            (d["lout"], state_block, block3),
            (d["ka"], keep_block, block3),
            *whole(*leav),
            (d["lin"], state_block, block3),
            (d["kb"], keep_block, block3),
            *whole(*d["arr"]),
            (d["rflow"], lane_block, block),
            (d["cflow"], lane_block, block),
            (d["dkk"], lane_block, block),
            *whole(d["par"], tril, ex, red),
        ]

    back_scratch = [
        pltpu.VMEM((GROUP + 8, width), f32),
        pltpu.VMEM((GROUP + 8, LANES), jnp.int32),
        pltpu.VMEM(half_in, f32),
        pltpu.VMEM(half_in, f32),
        pltpu.VMEM(half_in, bf16),
        pltpu.VMEM(half_in, bf16),
    ]

    def both_outs(cols, block):
        return [
            ((chunk, cols), bf16, (GROUP, cols), block),
            ((8, cols), f32, None, None),
            ((8, cols), f32, None, None),
        ]

    early_rev = lambda u: (count - 1 - jnp.minimum(u, count - 1), 0)
    late_rev = lambda u: (count - 1 - jnp.maximum(u - count, 0), 0)
    early_rev3 = lambda u: (count - 1 - jnp.minimum(u, count - 1), 0, 0)
    late_rev3 = lambda u: (count - 1 - jnp.maximum(u - count, 0), 0, 0)
    outs = run(
        functools.partial(turn_kernel, seqs, parts, count),
        (2 * count,),
        [
            *[(d["dbi"], lane_block, early_rev) for d in halves],
            *[(d["dci_c"], lane_block, early_rev) for d in halves],
            (dcin, lane_block, early_rev),
            (co_bc, map_block, early_rev),
            (ci_bc, map_block, early_rev),
            (age, lane_block, early_rev),
            (taps_bc, None, None),
            *[(d["val"], half_in, early_rev) for d in halves],
            *[(d["pre"], lane_block, early_rev) for d in halves],
            *[(d["cum"], lane_block, early_rev) for d in halves],
            *[(d["lout"], state_block, early_rev3) for d in halves],
            *[(d["ka"], keep_block, early_rev3) for d in halves],
            *whole(*leav, ex),
            *back_ins(1, late_rev, late_rev3),
            *whole(grad_o, share_z),
            (pieces, pl.ANY, None),
        ],
        both_outs(2 * LANES, early_rev)
        + [((32, 2 * LANES), f32, None, None), ((8, 2 * LANES), f32, None, None)]
        + both_outs(width, late_rev)
        + [
            ((chunk, LANES), bf16, lane_block, late_rev),
            ((32, width), f32, None, None),
            ((8, width), f32, None, None),
            ((8, LANES), f32, None, None),
            ((8, LANES), f32, None, None),
            ((up16(share_rows), quarter), bf16, None, None),
            ((features, quarter), f32, None, None),
            ((batch, piece, tokens), bf16, pl.ANY, None),
        ],
        [
            pltpu.VMEM((GROUP + 8, 2 * LANES), f32),
            pltpu.VMEM((GROUP + 8, LANES), jnp.int32),
            pltpu.VMEM(lane_block, f32),
        ]
        + back_scratch
        + [pltpu.SemaphoreType.DMA((2, 4))]
        + PairScatter.scratch(seqs, share_rows, quarter)
        + PairGather.scratch(seqs, share_rows, quarter),
        flops=30_000_000_000,
        moved=40_000_000,
        collective=4,
    )
    dbc, tail_bc, head_bc, gw_bc, gb_bc = outs[:5]
    hb.update(zip(("dx", "tail", "head", "draw", "gw", "gb", "galog", "gdtb"), outs[5:13]))
    share, grad_z, layer_out = outs[13:]

    steps = 3 * tiles + 2 * count
    back_unit = lambda u: (count - 1 - jnp.clip(u - 2 * tiles, 0, count - 1), 0)
    back_unit3 = lambda u: (count - 1 - jnp.clip(u - 2 * tiles, 0, count - 1), 0, 0)
    out_unit = lambda u: (jnp.clip(u - 3 * tiles - count, 0, count - 1), 0)

    def grad_tile(u):
        first = lax.rem(jnp.clip(u - 1, 0, 2 * tiles - 1), tiles)
        third = jnp.clip(u - 2 * tiles - count, 0, tiles - 1)
        later = jnp.minimum(u // (2 * tiles + count), 1)
        return 0, (1 - later) * first + later * third

    ending = lambda *_: (chunk // 16 - 1, 0)
    small_pack = (16, features)
    packed_rows = share_rows + 4 * -(-24 // seqs) + 4
    input_grad, sum2, g_bc, small_sum, grad_out = run(
        functools.partial(late_kernel, seqs, parts, count, tiles),
        (steps,),
        [
            *back_ins(0, back_unit, back_unit3),
            (normed, (chunk, GROUP), grad_tile),
            *whole(hb["dx"], hb["tail"], hb["head"]),
            (hb["ci"], (16, width), ending),
            *whole(hb["par"], hb["draw"], hb["gw"], hb["gb"], hb["galog"], hb["gdtb"]),
            *whole(dbc, tail_bc, head_bc),
            (ci_bc, (16, 2 * LANES), ending),
            *whole(taps_bc, gw_bc, gb_bc),
            (ha["ci"], (16, width), ending),
            *whole(next_age, gskip, ggain_out, share),
            (hidc, (GROUP, features), out_unit),
            (cotx, (GROUP, features), out_unit),
            (gain_in, None, None),
            (dgate, wide, out_unit),
            *whole(*zs, bc_proj, *xs, ha["dtp"], hb["dtp"]),
        ],
        [
            ((batch, piece, tokens), bf16, None, None),
            ((features, quarter), f32, None, None),
            ((features, 2 * LANES), f32, None, None),
            ((32, features), f32, None, None),
            ((quarter, features), f32, None, None),
        ],
        back_scratch
        + [
            pltpu.VMEM((chunk, width), bf16),
            pltpu.VMEM((chunk, LANES), bf16),
            pltpu.VMEM(x_shape, f32),
            pltpu.VMEM(x_shape, bf16),
            pltpu.VMEM(small_pack, f32),
            pltpu.VMEM(small_pack, f32),
            pltpu.VMEM(x_shape, bf16),
            pltpu.VMEM(small_pack, f32),
            pltpu.VMEM((16, width), bf16),
            pltpu.VMEM((8, width), f32),
            pltpu.VMEM((8, width), f32),
            pltpu.VMEM((32, width), f32),
            pltpu.VMEM((8, width), f32),
            pltpu.VMEM((8, LANES), f32),
            pltpu.VMEM((8, LANES), f32),
            pltpu.VMEM((chunk, width), bf16),
            pltpu.VMEM((chunk, 2 * LANES), bf16),
            pltpu.VMEM(x_shape, f32),
            pltpu.VMEM(x_shape, bf16),
            pltpu.VMEM(x_shape, bf16),
            pltpu.VMEM(x_shape, bf16),
        ]
        + [pltpu.VMEM(small_pack, f32)] * 5
        + [
            pltpu.VMEM(x_shape, bf16),
            pltpu.VMEM((8, width), f32),
            pltpu.VMEM((8, 2 * LANES), f32),
            pltpu.VMEM((8, width), f32),
            pltpu.VMEM((features, 2 * LANES), f32),
            pltpu.VMEM((2, features // 4, 2 * LANES), bf16),
            pltpu.VMEM((2, features // 4, 2 * LANES), bf16),
            pltpu.VMEM((features // 4, 2 * LANES), bf16),
            pltpu.VMEM((features // 4, 2 * LANES), bf16),
            pltpu.VMEM((features // 4, 2 * LANES), f32),
            pltpu.VMEM((8, 2 * LANES), f32),
            pltpu.VMEM((4, 8, 2 * LANES), f32),
            pltpu.VMEM((4, seqs, up16(features // 4 // seqs), 2 * LANES), bf16),
            pltpu.VMEM((GROUP, features), f32),
            pltpu.VMEM((GROUP, features), bf16),
            pltpu.VMEM((count, 4, piece, GROUP), bf16),
            pltpu.VMEM((count, 4, piece, GROUP), bf16),
            pltpu.VMEM((8, features), f32),
            pltpu.VMEM((4, 8, LANES), f32),
            pltpu.VMEM((8, LANES), f32),
            pltpu.SemaphoreType.DMA((2, 3)),
            pltpu.SemaphoreType.DMA((2, 18)),
            pltpu.SemaphoreType.DMA((2, count, 4)),
        ]
        + PairGather.scratch(seqs, share_rows, quarter)
        + Scatter.scratch(seqs, packed_rows, quarter)
        + Gather.scratch(seqs, packed_rows, quarter)
        + Scatter.scratch(seqs, features // 4 // seqs, 2 * LANES)
        + Gather.scratch(seqs, features // 4 // seqs, 2 * LANES),
        flops=40_000_000_000,
        moved=60_000_000,
        collective=5,
    )
    vector = lambda size: ((1, size), f32, None, None)
    gi, g_dt, g_taps, g_bias, g_maps, g_maps_bias, g_step, g_log, g_skip, g_gain = run(
        functools.partial(unpack_kernel, quarter, heads),
        (1,),
        whole(small_sum),
        [
            vector(piece),
            ((heads, features), f32, None, None),
            ((4, quarter), f32, None, None),
            vector(quarter),
            ((4, 2 * LANES), f32, None, None),
            vector(2 * LANES),
            vector(heads),
            vector(heads),
            vector(heads),
            vector(quarter),
        ],
        prefetch=(meta,),
    )
    return (
        jnp.swapaxes(layer_out, 1, 2),
        jnp.swapaxes(input_grad, 1, 2),
        gi[0],
        grad_z,
        sum2,
        g_bc,
        g_dt.T,
        g_taps.T,
        g_bias[0],
        g_maps.T,
        g_maps_bias[0],
        g_step[0],
        g_log[0],
        g_skip[0],
        g_gain[0],
        grad_out,
    )


def solution(mesh):
    return jax.shard_map(
        shards,
        mesh=mesh,
        in_specs=(
            P(None, "seq", None),
            P(None, "seq", "head"),
            P(),
            P(None, "head"),
            P(None, "head"),
            P(),
            P(None, "head"),
            P("head", None),
            P("head"),
            P(),
            P(),
            P("head"),
            P("head"),
            P("head"),
            P("head"),
            P("head", None),
            P(),
        ),
        out_specs=(
            P(None, "seq", "head"),
            P(None, "seq", "head"),
            P("head"),
            P(None, "head"),
            P(None, "head"),
            P(),
            P(None, "head"),
            P("head", None),
            P("head"),
            P(),
            P(),
            P("head"),
            P("head"),
            P("head"),
            P("head"),
            P("head", None),
        ),
        check_vma=False,
    )
```

profile of v0, /device:TPU:0, one launch (start us, length us, event | category | flops | bytes accessed | tf_op | source)
XLA Modules:
  0.0 280.2 jit_solution(310837895924183833)
XLA Ops:
  0.7 0.7 constant_dynamic-update-slice_fusion.4
  1.3 0.7 constant_dynamic-update-slice_fusion.3
  2.0 0.8 constant_dynamic-update-slice_fusion.2
  2.8 0.7 constant_dynamic-update-slice_fusion.1
  3.5 0.7 constant_dynamic-update-slice_fusion
  4.2 0.0 copy-start.6
  4.2 0.6 copy-done.6
  4.8 69.7 %shard_map.315 = (bf16[1024,768]{1,0:T(8,128)(2,1)}, bf16[1024,256]{1,0:T(8,128)(2,1)}, s32[1024,128]{1,0:T(8,128)}, s32[8,1024]{1,0:T(8,128)}, s32[8,128]{1,0:T...) custom-call(bf16[2,2048,768]{2,1,0:T(8,128)(2,1)} %hid.3, ...), custom_call_target="tpu_custom_call" | custom-call | flops 40000000000 | bytes 50000000 | tf_op jit(solution)/shard_map/pallas_call | solution.py:92
  74.5 39.3 %shard_map.316 = (bf16[4,192,1024]{2,1,0:T(8,128)(2,1)}, bf16[1024,768]{1,0:T(8,128)(2,1)}, bf16[1024,1536]{1,0:T(8,128)(2,1)}, bf16[1024,768]{1,0:T(8,128)(2,1)...) custom-call(s32[1]{0:T(128)} %bitcast.5.meta.me, ...), custom_call_target="tpu_custom_call" | custom-call | flops 30000001024 | bytes 50000000 | tf_op jit(solution)/shard_map/pallas_call | solution.py:92
  113.8 44.9 %shard_map.317 = (f32[1024,768]{1,0:T(8,128)}, f32[1024,128]{1,0:T(8,128)}, f32[1024,128]{1,0:T(8,128)}, f32[1024,128]{1,0:T(8,128)}, f32[1024,128]{1,0:T(8,128)...) custom-call(bf16[1024,768]{1,0:T(8,128)(2,1)} %get-tuple-element.127, ...), custom_call_target="tpu_custom_call" | custom-call | flops 30000001024 | bytes 40000000 | tf_op jit(solution)/shard_map/pallas_call | solution.py:92
  158.7 32.5 %shard_map.318 = (bf16[1024,256]{1,0:T(8,128)(2,1)}, f32[8,256]{1,0:T(8,128)}, f32[8,256]{1,0:T(8,128)}, f32[32,256]{1,0:T(8,128)}, f32[8,256]{1,0:T(8,128)}, /*...) custom-call(f32[1024,128]{1,0:T(8,128)} %get-tuple-element.169.refs_, ...), custom_call_target="tpu_custom_call" | custom-call | flops 30000001024 | bytes 40000000 | tf_op jit(solution)/shard_map/pallas_call | solution.py:92
  191.3 0.0 copy-start
  191.3 75.8 %shard_map.319 = (bf16[2,192,2048]{2,1,0:T(8,128)(2,1)}, f32[768,384]{1,0:T(8,128)}, f32[768,256]{1,0:T(8,128)}, f32[32,768]{1,0:T(8,128)}, f32[384,768]{1,0:T(8,128)}) custom-call(bf16[1024,768]{1,0:T(8,128)(2,1)} %get-tuple-element.143.val_a.refs_9_.refs_0_, bf16[1024,1536]{1,0:T(8,128)(2,1)} %get-tuple-element.160.dssd.refs_23_.refs_1_, ...), custom_call_target="tpu_custom_call" | custom-call | flops 40000000000 | bytes 60000000 | tf_op jit(solution)/shard_map/pallas_call | solution.py:92
  267.1 1.6 shard_map.320
  268.6 1.3 reduce
  269.9 1.3 reduce.1
  271.2 0.0 copy-done
  271.2 0.0 copy-start.1
  271.2 1.1 copy.47
  272.3 0.8 copy-done.1
  273.2 0.0 copy-start.2
  273.2 1.1 copy.48
  274.3 0.7 copy-done.2
  275.0 0.0 copy-start.4
  275.0 1.0 copy.49
  276.0 0.7 copy-done.4
  276.7 0.0 copy-start.5
  276.7 0.0 copy-start.3
  276.7 1.0 copy.50
  277.7 0.5 copy-done.5
  278.3 0.9 copy.51
  279.2 0.0 copy-done.3
  279.2 1.0 copy.52
  (1 shorter events, 0.0 us)
Async XLA Ops:
  4.2 0.6 copy-start.6
  191.3 79.9 %copy-start = (bf16[2,192,2048]{2,1,0:T(8,128)(2,1)S(1)}, bf16[2,192,2048]{2,1,0:T(8,128)(2,1)}, u32[]{:S(2)}) copy-start(bf16[2,192,2048]{2,1,0:T(8,128)(2,1)} %get-tuple-element.191) | copy-start | bytes 4718596
  271.2 2.0 copy-start.1
  273.2 1.8 copy-start.2
  275.0 1.7 copy-start.4
  276.7 1.6 copy-start.5
  276.7 2.4 copy-start.3
where the time goes:
time: 285 us; the launch traced here: 280 us
  Pallas kernels  264 us (93%)
  local copies, waits for them, and re-layouts  12.3 us (4%)
  other arithmetic  3.32 us (1%)
    pallas_call x6, Pallas kernels, run(): pl.pallas_call(kernel, grid_spec=pltpu.PrefetchScalarGridSpec(num_scalar_...  264 us
    unnamed x23, local copies, waits for them, and re-layouts  11.6 us

commit v1 on v0

--- a/solution.py
+++ b/solution.py
@@ -471,7 +471,7 @@
 
 
 def forward_kernel(
-    n, parts, count, hid, tail_rows, edge_near, starts, vecs, taps_x, dt_own, x_own, z_own, o_own, bc, taps_bc,
+    n, parts, count, hid, tail_rows, edge_near, starts, bias_x, gain_x, head_vecs, gain_in, bias_maps, taps_x, dt_own, x_own, z_own, o_own, bc, taps_bc,
     tril, ex, cotangent,
     normed, ci_bc, age, ager, next_age, gain_out, x_near, x_far, x_far_near, z_near, z_far, z_far_near,
     o_near, o_far, o_far_near, cot_near, cot_across, cot_corner, co_bc, bmat, cmat, *refs,
@@ -517,19 +517,16 @@
     def _():
         small_s[...] = jnp.zeros_like(small_s)
         small_s[0:4, 0:part] = taps_x[...]
-        tiles = part // LANES
-        for k in range(tiles):
+        for k in range(part // LANES):
             cols = slice(k * LANES, (k + 1) * LANES)
-            small_s[4:5, cols] = vecs[k : k + 1]
-            small_s[5:6, cols] = vecs[tiles + k : tiles + k + 1]
-        small_s[6:7, 0:LANES] = vecs[2 * tiles : 2 * tiles + 1]
+            small_s[4:5, cols] = bias_x[k : k + 1]
+            small_s[5:6, cols] = gain_x[k : k + 1]
+        small_s[6:7, 0:LANES] = head_vecs[...]
         small_s[8 : 8 + nh] = dt_own[...].astype(f32)
-        at = 2 * tiles + 2
         for k in range(features // LANES):
-            gain[0:1, k * LANES : (k + 1) * LANES] = vecs[at + k : at + k + 1]
-        at = at + features // LANES
+            gain[0:1, k * LANES : (k + 1) * LANES] = gain_in[k : k + 1]
         for k in range(2):
-            bias_bc[0:1, k * LANES : (k + 1) * LANES] = vecs[at + k : at + k + 1]
+            bias_bc[0:1, k * LANES : (k + 1) * LANES] = bias_maps[k : k + 1]
         gain_out[...] = jnp.broadcast_to(gain[0:1], gain_out.shape)
         edge_far[...] = jnp.zeros_like(edge_far)
         meet(heads[1:], n)
@@ -1733,16 +1730,22 @@
 
 
 def unpack_kernel(
-    quarter, heads, me, small, gi, dt, taps, bias, maps, maps_bias, step, log, skip, gain
+    quarter, heads, me, small, *refs
 ):
+    large, refs = refs[:6], refs[6:]
+    (gi, dt, taps, bias, maps, maps_bias, step, log, skip, gain), refs = refs[:10], refs[10:]
+    for a, b in zip(large, refs):
+        b[...] = a[...]
     features = small.shape[1]
     piece = gi.shape[1]
     row = pltpu.roll(small[24:32], lax.rem(features - me[0] * piece, features), 1)
     gi[...] = row[0:1, :piece]
     dt[...] = small[8 : 8 + heads]
     taps[...] = small[0:4, :quarter]
-    bias[...] = small[4:5, :quarter]
-    gain[...] = small[5:6, :quarter]
+    for k in range(quarter // LANES):
+        cols = slice(k * LANES, (k + 1) * LANES)
+        bias[k : k + 1] = small[4:5, cols]
+        gain[k : k + 1] = small[5:6, cols]
     maps[...] = small[16:20, : 2 * LANES]
     maps_bias[...] = small[20:21, : 2 * LANES]
     row = jnp.broadcast_to(small[6:7, 0:LANES], (8, LANES))
@@ -1803,15 +1806,8 @@
     def whole(*arrays):
         return [(a, None, None) for a in arrays]
 
-    vecs = jnp.concatenate(
-        [
-            conv_x_bias,
-            out_norm_gain,
-            jnp.pad(jnp.concatenate([dt_bias, a_log, d_skip]), (0, 2 * LANES - 3 * heads)),
-            input_norm_scale_gain,
-            conv_bc_bias,
-        ]
-    ).reshape(-1, LANES)
+    by_lanes = lambda x: x.reshape(-1, LANES)
+    head_vecs = jnp.pad(jnp.concatenate([dt_bias, a_log, d_skip]), (0, LANES - 3 * heads))[None]
     front_scratch = [
         pltpu.VMEM((GROUP + 8, width), f32),
         pltpu.VMEM((LANES, width), f32),
@@ -1875,7 +1871,8 @@
             ),
             (hidden_in, (1, 16, features), lambda u: (own_head() // parts, tokens // 16 - 1, 0)),
             (hidden_in, (1, 16, features), lambda u: (own_head() // parts, chunk // 16 - 1, 0)),
-            *whole(doc_starts, vecs, conv_x_weight.T, dt_proj.T, x_proj, z_proj, out_proj, bc_proj, taps_bc, tril, ex),
+            *whole(doc_starts, by_lanes(conv_x_bias), by_lanes(out_norm_gain), head_vecs),
+            *whole(by_lanes(input_norm_scale_gain), by_lanes(conv_bc_bias), conv_x_weight.T, dt_proj.T, x_proj, z_proj, out_proj, bc_proj, taps_bc, tril, ex),
             (cotangent, pl.ANY, None),
         ],
         [
@@ -2236,24 +2233,35 @@
         collective=5,
     )
     vector = lambda size: ((1, size), f32, None, None)
-    gi, g_dt, g_taps, g_bias, g_maps, g_maps_bias, g_step, g_log, g_skip, g_gain = run(
+    large = (layer_out, input_grad, grad_z, sum2, g_bc, grad_out)
+
+    def in_blocks(x):
+        if x.ndim == 3:
+            return x.shape[:2] + (x.shape[2] // 4,), lambda i, *_: (0, 0, i)
+        return (x.shape[0] // 4, x.shape[1]), lambda i, *_: (i, 0)
+
+    by_rows = ((quarter // LANES, LANES), f32, None, None)
+    outs = run(
         functools.partial(unpack_kernel, quarter, heads),
-        (1,),
-        whole(small_sum),
+        (4,),
+        whole(small_sum) + [(a, *in_blocks(a)) for a in large],
         [
             vector(piece),
             ((heads, features), f32, None, None),
             ((4, quarter), f32, None, None),
-            vector(quarter),
+            by_rows,
             ((4, 2 * LANES), f32, None, None),
             vector(2 * LANES),
             vector(heads),
             vector(heads),
             vector(heads),
-            vector(quarter),
-        ],
+            by_rows,
+        ]
+        + [(a.shape, a.dtype, *in_blocks(a)) for a in large],
         prefetch=(meta,),
     )
+    gi, g_dt, g_taps, g_bias, g_maps, g_maps_bias, g_step, g_log, g_skip, g_gain = outs[:10]
+    layer_out, input_grad, grad_z, sum2, g_bc, grad_out = outs[10:]
     return (
         jnp.swapaxes(layer_out, 1, 2),
         jnp.swapaxes(input_grad, 1, 2),
@@ -2263,13 +2271,13 @@
         g_bc,
         g_dt.T,
         g_taps.T,
-        g_bias[0],
+        g_bias.reshape(quarter),
         g_maps.T,
         g_maps_bias[0],
         g_step[0],
         g_log[0],
         g_skip[0],
-        g_gain[0],
+        g_gain.reshape(quarter),
         grad_out,
     )
 

time: 285 us -> 275 us (0.965)
  local copies, waits for them, and re-layouts: 12.3 us -> 0 us
  Pallas kernels: 264 us -> 269 us
    unnamed x23 -> x0, local copies, waits for them, and re-layouts: 11.6 us -> none
    pallas_call x6, Pallas kernels: 264 us -> 269 us  [run(): pl.pallas_call(kernel, grid_spec=pltpu.PrefetchScalarGridSpec(num_scalar_...]
where the time goes in v1:
time: 275 us; the launch traced here: 271 us
  Pallas kernels  269 us (98%)
    pallas_call x6, Pallas kernels, run(): pl.pallas_call(kernel, grid_spec=pltpu.PrefetchScalarGridSpec(num_scalar_...  269 us

profile of v1, /device:TPU:0, one launch (start us, length us, event | category | flops | bytes accessed | tf_op | source)
XLA Modules:
  0.0 271.1 jit_solution(4160709692120138268)
XLA Ops:
  0.7 1.3 fusion.head_vecs
  1.9 69.7 %shard_map.315 = (bf16[1024,768]{1,0:T(8,128)(2,1)}, bf16[1024,256]{1,0:T(8,128)(2,1)}, s32[1024,128]{1,0:T(8,128)}, s32[8,1024]{1,0:T(8,128)}, s32[8,128]{1,0:T...) custom-call(bf16[2,2048,768]{2,1,0:T(8,128)(2,1)} %hid.3, ...), custom_call_target="tpu_custom_call" | custom-call | flops 40000000000 | bytes 50000000 | tf_op jit(solution)/shard_map/pallas_call | solution.py:92
  71.7 39.3 %shard_map.316 = (bf16[4,192,1024]{2,1,0:T(8,128)(2,1)}, bf16[1024,768]{1,0:T(8,128)(2,1)}, bf16[1024,1536]{1,0:T(8,128)(2,1)}, bf16[1024,768]{1,0:T(8,128)(2,1)...) custom-call(s32[1]{0:T(128)} %bitcast.meta.me, ...), custom_call_target="tpu_custom_call" | custom-call | flops 30000001024 | bytes 50000000 | tf_op jit(solution)/shard_map/pallas_call | solution.py:92
  111.0 45.0 %shard_map.317 = (f32[1024,768]{1,0:T(8,128)}, f32[1024,128]{1,0:T(8,128)}, f32[1024,128]{1,0:T(8,128)}, f32[1024,128]{1,0:T(8,128)}, f32[1024,128]{1,0:T(8,128)...) custom-call(bf16[1024,768]{1,0:T(8,128)(2,1)} %get-tuple-element.134, ...), custom_call_target="tpu_custom_call" | custom-call | flops 30000001024 | bytes 40000000 | tf_op jit(solution)/shard_map/pallas_call | solution.py:92
  156.0 32.5 %shard_map.318 = (bf16[1024,256]{1,0:T(8,128)(2,1)}, f32[8,256]{1,0:T(8,128)}, f32[8,256]{1,0:T(8,128)}, f32[32,256]{1,0:T(8,128)}, f32[8,256]{1,0:T(8,128)}, /*...) custom-call(f32[1024,128]{1,0:T(8,128)} %get-tuple-element.185.refs_, ...), custom_call_target="tpu_custom_call" | custom-call | flops 30000001024 | bytes 40000000 | tf_op jit(solution)/shard_map/pallas_call | solution.py:92
  188.5 75.7 %shard_map.319 = (bf16[2,192,2048]{2,1,0:T(8,128)(2,1)}, f32[768,384]{1,0:T(8,128)}, f32[768,256]{1,0:T(8,128)}, f32[32,768]{1,0:T(8,128)}, f32[384,768]{1,0:T(8,128)}) custom-call(bf16[1024,768]{1,0:T(8,128)(2,1)} %get-tuple-element.133.val_a.refs_9_.refs_0_, bf16[1024,1536]{1,0:T(8,128)(2,1)} %get-tuple-element.163.dssd.refs_23_.refs_1_, ...), custom_call_target="tpu_custom_call" | custom-call | flops 40000000000 | bytes 60000000 | tf_op jit(solution)/shard_map/pallas_call | solution.py:92
  264.3 6.6 %shard_map.320 = (f32[1,192]{1,0:T(1,128)}, f32[6,768]{1,0:T(8,128)}, f32[4,384]{1,0:T(4,128)}, f32[3,128]{1,0:T(4,128)}, f32[4,256]{1,0:T(4,128)}, /*index=5*/f...) custom-call(s32[1]{0:T(128)} %bitcast.meta.me, ...), custom_call_target="tpu_custom_call" | custom-call | tf_op jit(solution)/shard_map/pallas_call | solution.py:92

commit v2 on v1

--- a/solution.py
+++ b/solution.py
@@ -897,12 +897,12 @@
     @pl.when(u == 3 * tiles)
     def _():
         swap(1, 0).start()
+        states.scan()
         cross_after(1)
 
     @pl.when(v == 0)
     def _():
         swap(1, 1).start()
-        states.scan()
 
     part = keep.shape[3]
     rows = pl.ds(pl.multiple_of(lax.rem(u, tiles) * GROUP, GROUP), GROUP)
@@ -923,7 +923,7 @@
     def _():
         pairs_unit(val_b, dssd, bmat, cmat, ager, pre_b, cum_b, dvi_b, dbi_b, dci_b, rflow_b, cflow_b, rft)
 
-    pl.when(u == 1)(states.combine)
+    pl.when(u == 0)(states.combine)
 
     pl.when(v == 2 * count - 3)(sums.middle)
 

time: 275 us -> 277 us (level)
  no operation moved by 1% of the time
where the time goes in v2:
time: 277 us; the launch traced here: 273 us
  Pallas kernels  271 us (98%)
    pallas_call x6, Pallas kernels, run(): pl.pallas_call(kernel, grid_spec=pltpu.PrefetchScalarGridSpec(num_scalar_...  271 us

profile of v2, /device:TPU:0, one launch (start us, length us, event | category | flops | bytes accessed | tf_op | source)
XLA Modules:
  0.0 272.7 jit_solution(16642441467196080254)
XLA Ops:
  0.7 1.3 fusion.head_vecs
  1.9 69.7 %shard_map.315 = (bf16[1024,768]{1,0:T(8,128)(2,1)}, bf16[1024,256]{1,0:T(8,128)(2,1)}, s32[1024,128]{1,0:T(8,128)}, s32[8,1024]{1,0:T(8,128)}, s32[8,128]{1,0:T...) custom-call(bf16[2,2048,768]{2,1,0:T(8,128)(2,1)} %hid.3, ...), custom_call_target="tpu_custom_call" | custom-call | flops 40000000000 | bytes 50000000 | tf_op jit(solution)/shard_map/pallas_call | solution.py:92
  71.7 39.3 %shard_map.316 = (bf16[4,192,1024]{2,1,0:T(8,128)(2,1)}, bf16[1024,768]{1,0:T(8,128)(2,1)}, bf16[1024,1536]{1,0:T(8,128)(2,1)}, bf16[1024,768]{1,0:T(8,128)(2,1)...) custom-call(s32[1]{0:T(128)} %bitcast.meta.me, ...), custom_call_target="tpu_custom_call" | custom-call | flops 30000001024 | bytes 50000000 | tf_op jit(solution)/shard_map/pallas_call | solution.py:92
  111.0 45.7 %shard_map.317 = (f32[1024,768]{1,0:T(8,128)}, f32[1024,128]{1,0:T(8,128)}, f32[1024,128]{1,0:T(8,128)}, f32[1024,128]{1,0:T(8,128)}, f32[1024,128]{1,0:T(8,128)...) custom-call(bf16[1024,768]{1,0:T(8,128)(2,1)} %get-tuple-element.134, ...), custom_call_target="tpu_custom_call" | custom-call | flops 30000001024 | bytes 40000000 | tf_op jit(solution)/shard_map/pallas_call | solution.py:92
  156.8 33.6 %shard_map.318 = (bf16[1024,256]{1,0:T(8,128)(2,1)}, f32[8,256]{1,0:T(8,128)}, f32[8,256]{1,0:T(8,128)}, f32[32,256]{1,0:T(8,128)}, f32[8,256]{1,0:T(8,128)}, /*...) custom-call(f32[1024,128]{1,0:T(8,128)} %get-tuple-element.185.refs_, ...), custom_call_target="tpu_custom_call" | custom-call | flops 30000001024 | bytes 40000000 | tf_op jit(solution)/shard_map/pallas_call | solution.py:92
  190.4 75.5 %shard_map.319 = (bf16[2,192,2048]{2,1,0:T(8,128)(2,1)}, f32[768,384]{1,0:T(8,128)}, f32[768,256]{1,0:T(8,128)}, f32[32,768]{1,0:T(8,128)}, f32[384,768]{1,0:T(8,128)}) custom-call(bf16[1024,768]{1,0:T(8,128)(2,1)} %get-tuple-element.133.val_a.refs_9_.refs_0_, bf16[1024,1536]{1,0:T(8,128)(2,1)} %get-tuple-element.163.dssd.refs_23_.refs_1_, ...), custom_call_target="tpu_custom_call" | custom-call | flops 40000000000 | bytes 60000000 | tf_op jit(solution)/shard_map/pallas_call | solution.py:92
  265.9 6.6 %shard_map.320 = (f32[1,192]{1,0:T(1,128)}, f32[6,768]{1,0:T(8,128)}, f32[4,384]{1,0:T(4,128)}, f32[3,128]{1,0:T(4,128)}, f32[4,256]{1,0:T(4,128)}, /*index=5*/f...) custom-call(s32[1]{0:T(128)} %bitcast.meta.me, ...), custom_call_target="tpu_custom_call" | custom-call | tf_op jit(solution)/shard_map/pallas_call | solution.py:92
